TPU v7x, 256 devices: a whole 4x4x8 slice. The times are simulated.
256 devices in a mesh: section: 8 (over y, x_hi), dp: 32 (over z, x_lo, core).
Axes of the slice: x: 4 (x_hi: 2, x_lo: 2; x = x_hi * 2 + x_lo), y: 4, z: 8, core: 2. Of those that a mesh axis runs over, the one named last changes fastest.
Arguments:
- block_hidden_input: bfloat16 [4, 1024, 8192], P(None, 'dp'), may hold values from -6 to 6
- cached_score_gradient: float32 [4, 32], P(None, 'dp'), may hold values from -24 to 24
- value_projection: bfloat16 [8, 8192, 512], P('section', 'dp'), may hold values from -0.0625 to 0.0625
- output_projection: bfloat16 [8, 512, 8192], P('section', None, 'dp'), may hold values from -0.25 to 0.25
- adapter_down_factor: bfloat16 [8, 8192, 64], P('section', 'dp'), may hold values from -0.0625 to 0.0625
- adapter_up_factor: bfloat16 [8, 64, 512], P('section'), may hold values from -0.75 to 0.75
- input_norm_gain: float32 [8, 8192], P('section'), may hold values from 0.5 to 1.5
- last_norm_gain: float32 [8192], replicated, may hold values from 0.5 to 1.5
- scoring_head_weight: float32 [8192], replicated, may hold values from -0.0625 to 0.0625
Outputs:
- grad_down: float32 [8, 8192, 64], P('section', 'dp')
- grad_up: float32 [8, 64, 512], P('section')
All inputs are finite; a program needn't handle non-finite values.
Results may differ from a plain program's by a relative error of at most 0.04.
Values may be sent and summed in bfloat16 or wider, within the bound.
A program may use at most 128 MiB of HBM per device.

v0:
```python
import jax
import jax.numpy as jnp
from jax import lax
from jax.sharding import PartitionSpec as P

ADAPTER_SCALE = 2.0
NORM_EPS = 1e-05


def shifted(value, axis, steps):
    count = lax.axis_size(axis)
    initial, last = (max(0, -steps), min(count, count - steps))
    return lax.ppermute(value, axis, [(source, source + steps) for source in range(initial, last)])


def normalize(hidden_state, input_norm_gain):
    values = hidden_state.astype(jnp.float32)
    factor = lax.rsqrt(jnp.mean(values * values, axis=-1, keepdims=True) + NORM_EPS)
    normalized_input = (values * factor * input_norm_gain).astype(jnp.bfloat16)
    return (values, factor, normalized_input)


def layer_forward_pass(
    hidden_state,
    input_norm_gain,
    value_projection,
    output_projection,
    adapter_down_factor,
    adapter_up_factor,
):
    values, factor, normalized_input = normalize(hidden_state, input_norm_gain)
    adapter_activation = jnp.dot(
        normalized_input, adapter_down_factor, preferred_element_type=jnp.float32
    ).astype(jnp.bfloat16)
    value_projected = jnp.dot(
        normalized_input, value_projection, preferred_element_type=jnp.float32
    )
    value_projected = value_projected + ADAPTER_SCALE * jnp.dot(
        adapter_activation, adapter_up_factor, preferred_element_type=jnp.float32
    )
    value_projected = value_projected.astype(jnp.bfloat16)
    layer_result = (
        values + jnp.dot(value_projected, output_projection, preferred_element_type=jnp.float32)
    ).astype(jnp.bfloat16)
    return (normalized_input, adapter_activation, layer_result)


def score_seed(hidden_state, last_norm_gain, scoring_head_weight, token_grads, length):
    values = hidden_state.astype(jnp.float32)
    factor = lax.rsqrt(jnp.mean(values * values, axis=-1, keepdims=True) + NORM_EPS)
    weighted = last_norm_gain * scoring_head_weight
    inner_sum = jnp.sum(values * weighted, axis=-1, keepdims=True)
    columns = values.shape[-1]
    seed_grad = factor * weighted - factor * factor * factor * inner_sum * values / columns
    return (seed_grad * token_grads / length).astype(jnp.bfloat16)


def layer_backward_pass(
    hidden_state,
    following_gradient,
    input_norm_gain,
    value_projection,
    output_projection,
    adapter_down_factor,
    adapter_up_factor,
    normalized_input,
    adapter_activation,
):
    values, factor, unused = normalize(hidden_state, input_norm_gain)
    value_gradient = jnp.einsum(
        "rd,kd->rk", following_gradient, output_projection, preferred_element_type=jnp.float32
    ).astype(jnp.bfloat16)
    up_factor_term = ADAPTER_SCALE * jnp.einsum(
        "rq,rk->qk", adapter_activation, value_gradient, preferred_element_type=jnp.float32
    )
    adapter_gradient = (
        ADAPTER_SCALE
        * jnp.einsum(
            "ts,ps->tp", value_gradient, adapter_up_factor, preferred_element_type=jnp.float32
        )
    ).astype(jnp.bfloat16)
    normalized_gradient = jnp.einsum(
        "rk,dk->rd", value_gradient, value_projection, preferred_element_type=jnp.float32
    )
    normalized_gradient = normalized_gradient + jnp.einsum(
        "hk,ik->hi", adapter_gradient, adapter_down_factor, preferred_element_type=jnp.float32
    )
    down_factor_term = jnp.einsum(
        "rd,rq->dq", normalized_input, adapter_gradient, preferred_element_type=jnp.float32
    )
    scaled = normalized_gradient * input_norm_gain
    inner_sum = jnp.sum(values * scaled, axis=-1, keepdims=True)
    columns = values.shape[-1]
    hidden_state_gradient = (
        factor * scaled - factor * factor * factor * inner_sum * values / columns
    )
    hidden_state_gradient = (following_gradient.astype(jnp.float32) + hidden_state_gradient).astype(
        jnp.bfloat16
    )
    return (hidden_state_gradient, down_factor_term, up_factor_term)


def per_device(
    block_hidden_input,
    cached_score_gradient,
    value_projection,
    output_projection,
    adapter_down_factor,
    adapter_up_factor,
    input_norm_gain,
    last_norm_gain,
    scoring_head_weight,
):
    section_index = lax.axis_index("section")
    section_count = lax.axis_size("section")
    last_section = section_count - 1
    block_total = block_hidden_input.shape[0]
    rows = block_hidden_input.shape[1]
    steps_total = block_total + section_count - 1
    value_full, down_full = (
        lax.all_gather(value_projection[0], "dp", axis=0, tiled=True),
        lax.all_gather(adapter_down_factor[0], "dp", axis=0, tiled=True),
    )
    out_full = lax.all_gather(output_projection[0], "dp", axis=1, tiled=True)
    complete_up_gradient = adapter_up_factor[0]
    layer_gain = input_norm_gain[0]

    def run_forward(hidden_state):
        return layer_forward_pass(
            hidden_state, layer_gain, value_full, out_full, down_full, complete_up_gradient
        )

    def blank_forward(hidden_state):
        return (
            jnp.zeros_like(hidden_state),
            jnp.zeros((rows, down_full.shape[1]), jnp.bfloat16),
            jnp.zeros_like(hidden_state),
        )

    inputs_init = jnp.zeros_like(block_hidden_input)
    carried_init = (
        jnp.zeros_like(block_hidden_input[0]),
        inputs_init,
        inputs_init,
        inputs_init,
        jnp.zeros((block_total, rows, down_full.shape[1]), jnp.bfloat16),
    )

    def forward_step(step_index, carried):
        incoming = carried[0]
        layer_inputs = carried[1]
        finals = carried[2]
        micro_index = step_index - section_index
        active = jnp.logical_and(micro_index >= 0, micro_index < block_total)
        slot_index = jnp.clip(micro_index, 0, block_total - 1)
        first_input = lax.dynamic_index_in_dim(block_hidden_input, slot_index, 0, keepdims=False)
        hidden_state = jnp.where(section_index == 0, first_input, incoming)
        normalized_input, adapter_activation, layer_result = lax.cond(
            active, run_forward, blank_forward, hidden_state
        )
        layer_inputs = jnp.where(
            active,
            lax.dynamic_update_index_in_dim(layer_inputs, hidden_state, slot_index, 0),
            layer_inputs,
        )
        finals = jnp.where(
            jnp.logical_and(active, section_index == last_section),
            lax.dynamic_update_index_in_dim(finals, layer_result, slot_index, 0),
            finals,
        )
        outgoing = shifted(layer_result, "section", 1)
        normed_all = jnp.where(
            active,
            lax.dynamic_update_index_in_dim(carried[3], normalized_input, slot_index, 0),
            carried[3],
        )
        lowrank_all = jnp.where(
            active,
            lax.dynamic_update_index_in_dim(carried[4], adapter_activation, slot_index, 0),
            carried[4],
        )
        return (outgoing, layer_inputs, finals, normed_all, lowrank_all)

    carried = lax.fori_loop(0, steps_total, forward_step, carried_init)
    layer_inputs = carried[1]
    finals = carried[2]

    def backward_step(step_index, state):
        incoming, total_down, total_up = state
        micro_index = step_index - (last_section - section_index)
        active = jnp.logical_and(micro_index >= 0, micro_index < block_total)
        slot_index = jnp.clip(micro_index, 0, block_total - 1)
        hidden_state = lax.dynamic_index_in_dim(layer_inputs, slot_index, 0, keepdims=False)
        final_field = lax.dynamic_index_in_dim(finals, slot_index, 0, keepdims=False)
        block_grad = lax.dynamic_index_in_dim(cached_score_gradient, slot_index, 0, keepdims=False)
        seed_grad = score_seed(final_field, last_norm_gain, scoring_head_weight, block_grad, rows)
        following_gradient = jnp.where(section_index == last_section, seed_grad, incoming)
        normalized_input = lax.dynamic_index_in_dim(carried[3], slot_index, 0, keepdims=False)
        adapter_activation = lax.dynamic_index_in_dim(carried[4], slot_index, 0, keepdims=False)

        def run_backward(operands):
            return layer_backward_pass(
                operands[0],
                operands[1],
                layer_gain,
                value_full,
                out_full,
                down_full,
                complete_up_gradient,
                operands[2],
                operands[3],
            )

        def blank_backward(operands):
            return (
                jnp.zeros_like(operands[1]),
                jnp.zeros_like(total_down),
                jnp.zeros_like(total_up),
            )

        hidden_state_gradient, down_factor_term, up_factor_term = lax.cond(
            active,
            run_backward,
            blank_backward,
            (hidden_state, following_gradient, normalized_input, adapter_activation),
        )
        outgoing = shifted(hidden_state_gradient, "section", -1)
        return (outgoing, total_down + down_factor_term, total_up + up_factor_term)

    state_init = (
        jnp.zeros_like(block_hidden_input[0]),
        jnp.zeros((value_full.shape[0], down_full.shape[1]), jnp.float32),
        jnp.zeros(complete_up_gradient.shape, jnp.float32),
    )
    state_done = lax.fori_loop(0, steps_total, backward_step, state_init)
    grad_down = lax.psum_scatter(
        state_done[1].astype(jnp.bfloat16), "dp", scatter_dimension=0, tiled=True
    ).astype(jnp.float32)
    grad_up = lax.psum(state_done[2].astype(jnp.bfloat16), "dp").astype(jnp.float32)
    return (grad_down[None], grad_up[None])


def solution(mesh):
    return jax.shard_map(
        per_device,
        mesh=mesh,
        in_specs=(
            P(None, "dp", None),
            P(None, "dp"),
            P("section", "dp", None),
            P("section", None, "dp"),
            P("section", "dp", None),
            P("section", None, None),
            P("section", None),
            P(),
            P(),
        ),
        out_specs=(P("section", "dp", None), P("section", None, None)),
        check_vma=False,
    )
```

profile of v0, /device:TPU:1, one launch (start us, length us, event | category | flops | bytes accessed | tf_op | source)
XLA Modules:
  0.0 1242.3 jit_solution(10478768724613203567)
XLA Ops:
  11.1 68.3 %all-gather.9.cloned.1.call-done = bf16[1,8192,64]{2,1,0:T(8,128)(2,1)} async-done(((bf16[1,256,64]{2,1,0:T(8,128)(2,1)}), bf16[1,8192,64]{2,1,0:T(8,128)(2,1)}) %all-gather.9.cloned.1.call-update) | async-done | bytes 1048592 | tf_op jit(solution)/shard_map/all_gather | solution.py:122
  79.3 73.9 %all-gather.7.cloned.1.call-done = bf16[1,8192,512]{2,1,0:T(8,128)(2,1)} async-done(((bf16[1,256,512]{2,1,0:T(8,128)(2,1)}), bf16[1,8192,512]{2,1,0:T(8,128)(2,1)}) %all-gather.7.cloned.1.call-update) | async-done | bytes 8388624 | tf_op jit(solution)/shard_map/all_gather | solution.py:121
  153.2 91.3 %all-gather.11.cloned.1.call-done = bf16[1,512,8192]{2,1,0:T(8,128)(2,1)} async-done(((bf16[1,512,256]{2,1,0:T(8,128)(2,1)}), bf16[1,512,8192]{2,1,0:T(8,128)(2,1)}) %all-gather.11.cloned.1.call-update) | async-done | bytes 8388624 | tf_op jit(solution)/shard_map/all_gather | solution.py:124
  249.8 285.5 %while.42 = (s32[]{:T(128)}, bf16[32,8192]{1,0:T(8,128)(2,1)S(1)}, bf16[4,32,8192]{2,1,0:T(8,128)(2,1)}, bf16[4,32,8192]{2,1,0:T(8,128)(2,1)}, bf16[4,32,8192]{2...) while((s32[]{:T(128)}, bf16[32,8192]{1,0:T(8,128)(2,1)S(1)}, ...), condition=%wide.region_4.5_spmd, body=%wide.region_0.4_spmd.sunk | while | flops 578342912 | bytes 30766768 | solution.py:184
  252.1 14.4 %conditional.5 = (bf16[32,8192]{1,0:T(8,128)(2,1)}, bf16[1,32,8192]{2,1,0:T(8,128)(2,1)S(1)}, bf16[1,32,8192]{2,1,0:T(8,128)(2,1)S(1)}, bf16[1,32,64]{2,1,0:T(8,128)(2,1)S(1)}) conditional(s32[]{:T(128)} %convert_element_type.128, () %tuple.115, (bf16[32,8192]{1,0:T(8,128)(2,1)S(1)}, f32[1,8192]{1,0:T(1,128)S(1)}, bf16[8192,512]{1,0:T(8,128)(2,1)}, ...), branch_computations={%region_1.1_spmd, %region_2.3_spmd} | conditional | flops 577292288 | bytes 22881112 | solution.py:158
  281.7 14.4 %conditional.5 = (bf16[32,8192]{1,0:T(8,128)(2,1)}, bf16[1,32,8192]{2,1,0:T(8,128)(2,1)S(1)}, bf16[1,32,8192]{2,1,0:T(8,128)(2,1)S(1)}, bf16[1,32,64]{2,1,0:T(8,128)(2,1)S(1)}) conditional(s32[]{:T(128)} %convert_element_type.128, () %tuple.115, (bf16[32,8192]{1,0:T(8,128)(2,1)S(1)}, f32[1,8192]{1,0:T(1,128)S(1)}, bf16[8192,512]{1,0:T(8,128)(2,1)}, ...), branch_computations={%region_1.1_spmd, %region_2.3_spmd} | conditional | flops 577292288 | bytes 22881112 | solution.py:158
  314.6 14.4 %conditional.5 = (bf16[32,8192]{1,0:T(8,128)(2,1)}, bf16[1,32,8192]{2,1,0:T(8,128)(2,1)S(1)}, bf16[1,32,8192]{2,1,0:T(8,128)(2,1)S(1)}, bf16[1,32,64]{2,1,0:T(8,128)(2,1)S(1)}) conditional(s32[]{:T(128)} %convert_element_type.128, () %tuple.115, (bf16[32,8192]{1,0:T(8,128)(2,1)S(1)}, f32[1,8192]{1,0:T(1,128)S(1)}, bf16[8192,512]{1,0:T(8,128)(2,1)}, ...), branch_computations={%region_1.1_spmd, %region_2.3_spmd} | conditional | flops 577292288 | bytes 22881112 | solution.py:158
  346.6 14.4 %conditional.5 = (bf16[32,8192]{1,0:T(8,128)(2,1)}, bf16[1,32,8192]{2,1,0:T(8,128)(2,1)S(1)}, bf16[1,32,8192]{2,1,0:T(8,128)(2,1)S(1)}, bf16[1,32,64]{2,1,0:T(8,128)(2,1)S(1)}) conditional(s32[]{:T(128)} %convert_element_type.128, () %tuple.115, (bf16[32,8192]{1,0:T(8,128)(2,1)S(1)}, f32[1,8192]{1,0:T(1,128)S(1)}, bf16[8192,512]{1,0:T(8,128)(2,1)}, ...), branch_computations={%region_1.1_spmd, %region_2.3_spmd} | conditional | flops 577292288 | bytes 22881112 | solution.py:158
  378.7 19.0 %collective-permute-start = (bf16[32,8192]{1,0:T(8,128)(2,1)}, bf16[32,8192]{1,0:T(8,128)(2,1)S(1)}, u32[]{:S(2)}, u32[]{:S(2)}) collective-permute-start(bf16[32,8192]{1,0:T(8,128)(2,1)} %get-tuple-element.1128), channel_id=1, source_target_pairs={{0,32},{32,64},{64,96},{96,128},{128,160},{160,192},{192,224},{1,3... | collective-permute-start | bytes 1572872 | tf_op jit(solution)/shard_map/while/body/eval_jaxpr/ppermute | solution.py:13
  425.3 19.9 %collective-permute-start = (bf16[32,8192]{1,0:T(8,128)(2,1)}, bf16[32,8192]{1,0:T(8,128)(2,1)S(1)}, u32[]{:S(2)}, u32[]{:S(2)}) collective-permute-start(bf16[32,8192]{1,0:T(8,128)(2,1)} %get-tuple-element.1128), channel_id=1, source_target_pairs={{0,32},{32,64},{64,96},{96,128},{128,160},{160,192},{192,224},{1,3... | collective-permute-start | bytes 1572872 | tf_op jit(solution)/shard_map/while/body/eval_jaxpr/ppermute | solution.py:13
  470.8 15.2 %collective-permute-start = (bf16[32,8192]{1,0:T(8,128)(2,1)}, bf16[32,8192]{1,0:T(8,128)(2,1)S(1)}, u32[]{:S(2)}, u32[]{:S(2)}) collective-permute-start(bf16[32,8192]{1,0:T(8,128)(2,1)} %get-tuple-element.1128), channel_id=1, source_target_pairs={{0,32},{32,64},{64,96},{96,128},{128,160},{160,192},{192,224},{1,3... | collective-permute-start | bytes 1572872 | tf_op jit(solution)/shard_map/while/body/eval_jaxpr/ppermute | solution.py:13
  511.2 17.7 %collective-permute-start = (bf16[32,8192]{1,0:T(8,128)(2,1)}, bf16[32,8192]{1,0:T(8,128)(2,1)S(1)}, u32[]{:S(2)}, u32[]{:S(2)}) collective-permute-start(bf16[32,8192]{1,0:T(8,128)(2,1)} %get-tuple-element.1128), channel_id=1, source_target_pairs={{0,32},{32,64},{64,96},{96,128},{128,160},{160,192},{192,224},{1,3... | collective-permute-start | bytes 1572872 | tf_op jit(solution)/shard_map/while/body/eval_jaxpr/ppermute | solution.py:13
  535.3 376.3 %while.43 = (s32[]{:T(128)}, bf16[32,8192]{1,0:T(8,128)(2,1)S(1)}, f32[8192,64]{0,1:T(8,128)}, f32[64,512]{1,0:T(8,128)S(1)}, s32[]{:T(128)}, /*index=5*/bf16[4,...) while((s32[]{:T(128)}, bf16[32,8192]{1,0:T(8,128)(2,1)S(1)}, ...), condition=%wide.region_12.13_spmd.clone, body=%wide.region_5.12_spmd.clone.sunk | while | flops 617206016 | bytes 72670688 | solution.py:235
  542.5 11.6 collective-permute-done.1
  562.9 16.4 %collective-permute-done.1 = bf16[32,8192]{1,0:T(8,128)(2,1)S(1)} collective-permute-done((bf16[32,8192]{1,0:T(8,128)(2,1)S(1)}, bf16[32,8192]{1,0:T(8,128)(2,1)S(1)}, u32[]{:S(2)}, u32[]{:S(2)}) %collective-permute-start.1) | collective-permute-done | bytes 524320 | tf_op jit(solution)/shard_map/while/body/eval_jaxpr/ppermute | solution.py:13
  605.2 18.9 %collective-permute-done.1 = bf16[32,8192]{1,0:T(8,128)(2,1)S(1)} collective-permute-done((bf16[32,8192]{1,0:T(8,128)(2,1)S(1)}, bf16[32,8192]{1,0:T(8,128)(2,1)S(1)}, u32[]{:S(2)}, u32[]{:S(2)}) %collective-permute-start.1) | collective-permute-done | bytes 524320 | tf_op jit(solution)/shard_map/while/body/eval_jaxpr/ppermute | solution.py:13
  650.1 16.3 %collective-permute-done.1 = bf16[32,8192]{1,0:T(8,128)(2,1)S(1)} collective-permute-done((bf16[32,8192]{1,0:T(8,128)(2,1)S(1)}, bf16[32,8192]{1,0:T(8,128)(2,1)S(1)}, u32[]{:S(2)}, u32[]{:S(2)}) %collective-permute-start.1) | collective-permute-done | bytes 524320 | tf_op jit(solution)/shard_map/while/body/eval_jaxpr/ppermute | solution.py:13
  675.2 110.7 %collective-permute-done.1 = bf16[32,8192]{1,0:T(8,128)(2,1)S(1)} collective-permute-done((bf16[32,8192]{1,0:T(8,128)(2,1)S(1)}, bf16[32,8192]{1,0:T(8,128)(2,1)S(1)}, u32[]{:S(2)}, u32[]{:S(2)}) %collective-permute-start.1) | collective-permute-done | bytes 524320 | tf_op jit(solution)/shard_map/while/body/eval_jaxpr/ppermute | solution.py:13
  789.9 15.3 %conditional.6 = (bf16[32,8192]{1,0:T(8,128)(2,1)S(1)}, f32[8192,64]{0,1:T(8,128)S(1)}, f32[64,512]{1,0:T(8,128)S(1)}) conditional(s32[]{:T(128)} %convert_element_type.130, () %tuple.120, (pred[]{:T(512)}, bf16[32,8192]{1,0:T(8,128)(2,1)S(1)}, bf16[32,8192]{1,0:T(8,128)(2,1)S(1)}, bf16[4,32,8192]{2,1,0:T(8,128)(2,1)}, s32[]{:T(128)}, ...), branch_computations={%region_8.8_spmd, %region_9.11_spmd} | conditional | flops 612683904 | bytes 62249020 | solution.py:221
  821.6 15.3 %conditional.6 = (bf16[32,8192]{1,0:T(8,128)(2,1)S(1)}, f32[8192,64]{0,1:T(8,128)S(1)}, f32[64,512]{1,0:T(8,128)S(1)}) conditional(s32[]{:T(128)} %convert_element_type.130, () %tuple.120, (pred[]{:T(512)}, bf16[32,8192]{1,0:T(8,128)(2,1)S(1)}, bf16[32,8192]{1,0:T(8,128)(2,1)S(1)}, bf16[4,32,8192]{2,1,0:T(8,128)(2,1)}, s32[]{:T(128)}, ...), branch_computations={%region_8.8_spmd, %region_9.11_spmd} | conditional | flops 612683904 | bytes 62249020 | solution.py:221
  853.2 15.3 %conditional.6 = (bf16[32,8192]{1,0:T(8,128)(2,1)S(1)}, f32[8192,64]{0,1:T(8,128)S(1)}, f32[64,512]{1,0:T(8,128)S(1)}) conditional(s32[]{:T(128)} %convert_element_type.130, () %tuple.120, (pred[]{:T(512)}, bf16[32,8192]{1,0:T(8,128)(2,1)S(1)}, bf16[32,8192]{1,0:T(8,128)(2,1)S(1)}, bf16[4,32,8192]{2,1,0:T(8,128)(2,1)}, s32[]{:T(128)}, ...), branch_computations={%region_8.8_spmd, %region_9.11_spmd} | conditional | flops 612683904 | bytes 62249020 | solution.py:221
  884.9 15.3 %conditional.6 = (bf16[32,8192]{1,0:T(8,128)(2,1)S(1)}, f32[8192,64]{0,1:T(8,128)S(1)}, f32[64,512]{1,0:T(8,128)S(1)}) conditional(s32[]{:T(128)} %convert_element_type.130, () %tuple.120, (pred[]{:T(512)}, bf16[32,8192]{1,0:T(8,128)(2,1)S(1)}, bf16[32,8192]{1,0:T(8,128)(2,1)S(1)}, bf16[4,32,8192]{2,1,0:T(8,128)(2,1)}, s32[]{:T(128)}, ...), branch_computations={%region_8.8_spmd, %region_9.11_spmd} | conditional | flops 612683904 | bytes 62249020 | solution.py:221
  915.0 204.3 %all-reduce.2.cloned.1.call-done = bf16[1,64,512]{2,1,0:T(8,128)(2,1)} async-done(((bf16[1,64,512]{2,1,0:T(8,128)(2,1)}), bf16[1,64,512]{2,1,0:T(8,128)(2,1)}) %all-reduce.2.cloned.1.call-update) | async-done | bytes 65552 | tf_op jit(solution)/shard_map/psum | solution.py:239
  1120.9 113.5 %reduce-scatter.2.cloned.1.call-done = bf16[256,64]{0,1:T(8,128)(2,1)} async-done(((bf16[8192,64]{0,1:T(8,128)(2,1)}), bf16[256,64]{0,1:T(8,128)(2,1)}) %reduce-scatter.2.cloned.1.call-update) | async-done | bytes 32784 | tf_op jit(solution)/shard_map/reduce_scatter | solution.py:236
  (311 shorter events, 438.3 us)
Async XLA Ops:
  7.2 72.2 %all-gather.9.cloned.1.call-start = ((), (), s32[]{:S(2)}) async-start(), calls=%async_computation.4 | async-start | bytes 2162688 | tf_op jit(solution)/shard_map/all_gather | solution.py:122
  8.7 144.5 %all-gather.7.cloned.1.call-start = ((), (), s32[]{:S(2)}) async-start(), calls=%async_computation.3 | async-start | bytes 8650752 | tf_op jit(solution)/shard_map/all_gather | solution.py:121
  9.5 235.0 %all-gather.11.cloned.1.call-start = ((), (), s32[]{:S(2)}) async-start(), calls=%async_computation.5 | async-start | bytes 8650752 | tf_op jit(solution)/shard_map/all_gather | solution.py:124
  10.2 1109.2 %all-reduce.2.cloned.1.call-start = ((), (), s32[]{:S(2)}) async-start(), calls=%async_computation.2 | async-start | bytes 131072 | tf_op jit(solution)/shard_map/psum | solution.py:239
  266.5 13.0 %collective-permute-start = (bf16[32,8192]{1,0:T(8,128)(2,1)}, bf16[32,8192]{1,0:T(8,128)(2,1)S(1)}, u32[]{:S(2)}, u32[]{:S(2)}) collective-permute-start(bf16[32,8192]{1,0:T(8,128)(2,1)} %get-tuple-element.1128), channel_id=1, source_target_pairs={{0,32},{32,64},{64,96},{96,128},{128,160},{160,192},{192,224},{1,3... | collective-permute-start | bytes 1572872 | tf_op jit(solution)/shard_map/while/body/eval_jaxpr/ppermute | solution.py:13
  296.1 16.3 %collective-permute-start = (bf16[32,8192]{1,0:T(8,128)(2,1)}, bf16[32,8192]{1,0:T(8,128)(2,1)S(1)}, u32[]{:S(2)}, u32[]{:S(2)}) collective-permute-start(bf16[32,8192]{1,0:T(8,128)(2,1)} %get-tuple-element.1128), channel_id=1, source_target_pairs={{0,32},{32,64},{64,96},{96,128},{128,160},{160,192},{192,224},{1,3... | collective-permute-start | bytes 1572872 | tf_op jit(solution)/shard_map/while/body/eval_jaxpr/ppermute | solution.py:13
  329.1 15.4 %collective-permute-start = (bf16[32,8192]{1,0:T(8,128)(2,1)}, bf16[32,8192]{1,0:T(8,128)(2,1)S(1)}, u32[]{:S(2)}, u32[]{:S(2)}) collective-permute-start(bf16[32,8192]{1,0:T(8,128)(2,1)} %get-tuple-element.1128), channel_id=1, source_target_pairs={{0,32},{32,64},{64,96},{96,128},{128,160},{160,192},{192,224},{1,3... | collective-permute-start | bytes 1572872 | tf_op jit(solution)/shard_map/while/body/eval_jaxpr/ppermute | solution.py:13
  361.1 14.5 %collective-permute-start = (bf16[32,8192]{1,0:T(8,128)(2,1)}, bf16[32,8192]{1,0:T(8,128)(2,1)S(1)}, u32[]{:S(2)}, u32[]{:S(2)}) collective-permute-start(bf16[32,8192]{1,0:T(8,128)(2,1)} %get-tuple-element.1128), channel_id=1, source_target_pairs={{0,32},{32,64},{64,96},{96,128},{128,160},{160,192},{192,224},{1,3... | collective-permute-start | bytes 1572872 | tf_op jit(solution)/shard_map/while/body/eval_jaxpr/ppermute | solution.py:13
  378.7 27.0 %collective-permute-start = (bf16[32,8192]{1,0:T(8,128)(2,1)}, bf16[32,8192]{1,0:T(8,128)(2,1)S(1)}, u32[]{:S(2)}, u32[]{:S(2)}) collective-permute-start(bf16[32,8192]{1,0:T(8,128)(2,1)} %get-tuple-element.1128), channel_id=1, source_target_pairs={{0,32},{32,64},{64,96},{96,128},{128,160},{160,192},{192,224},{1,3... | collective-permute-start | bytes 1572872 | tf_op jit(solution)/shard_map/while/body/eval_jaxpr/ppermute | solution.py:13
  408.9 13.3 %collective-permute-start = (bf16[32,8192]{1,0:T(8,128)(2,1)}, bf16[32,8192]{1,0:T(8,128)(2,1)S(1)}, u32[]{:S(2)}, u32[]{:S(2)}) collective-permute-start(bf16[32,8192]{1,0:T(8,128)(2,1)} %get-tuple-element.1128), channel_id=1, source_target_pairs={{0,32},{32,64},{64,96},{96,128},{128,160},{160,192},{192,224},{1,3... | collective-permute-start | bytes 1572872 | tf_op jit(solution)/shard_map/while/body/eval_jaxpr/ppermute | solution.py:13
  425.3 26.3 %collective-permute-start = (bf16[32,8192]{1,0:T(8,128)(2,1)}, bf16[32,8192]{1,0:T(8,128)(2,1)S(1)}, u32[]{:S(2)}, u32[]{:S(2)}) collective-permute-start(bf16[32,8192]{1,0:T(8,128)(2,1)} %get-tuple-element.1128), channel_id=1, source_target_pairs={{0,32},{32,64},{64,96},{96,128},{128,160},{160,192},{192,224},{1,3... | collective-permute-start | bytes 1572872 | tf_op jit(solution)/shard_map/while/body/eval_jaxpr/ppermute | solution.py:13
  454.8 12.8 %collective-permute-start = (bf16[32,8192]{1,0:T(8,128)(2,1)}, bf16[32,8192]{1,0:T(8,128)(2,1)S(1)}, u32[]{:S(2)}, u32[]{:S(2)}) collective-permute-start(bf16[32,8192]{1,0:T(8,128)(2,1)} %get-tuple-element.1128), channel_id=1, source_target_pairs={{0,32},{32,64},{64,96},{96,128},{128,160},{160,192},{192,224},{1,3... | collective-permute-start | bytes 1572872 | tf_op jit(solution)/shard_map/while/body/eval_jaxpr/ppermute | solution.py:13
  470.8 21.6 %collective-permute-start = (bf16[32,8192]{1,0:T(8,128)(2,1)}, bf16[32,8192]{1,0:T(8,128)(2,1)S(1)}, u32[]{:S(2)}, u32[]{:S(2)}) collective-permute-start(bf16[32,8192]{1,0:T(8,128)(2,1)} %get-tuple-element.1128), channel_id=1, source_target_pairs={{0,32},{32,64},{64,96},{96,128},{128,160},{160,192},{192,224},{1,3... | collective-permute-start | bytes 1572872 | tf_op jit(solution)/shard_map/while/body/eval_jaxpr/ppermute | solution.py:13
  495.5 12.5 %collective-permute-start = (bf16[32,8192]{1,0:T(8,128)(2,1)}, bf16[32,8192]{1,0:T(8,128)(2,1)S(1)}, u32[]{:S(2)}, u32[]{:S(2)}) collective-permute-start(bf16[32,8192]{1,0:T(8,128)(2,1)} %get-tuple-element.1128), channel_id=1, source_target_pairs={{0,32},{32,64},{64,96},{96,128},{128,160},{160,192},{192,224},{1,3... | collective-permute-start | bytes 1572872 | tf_op jit(solution)/shard_map/while/body/eval_jaxpr/ppermute | solution.py:13
  511.2 24.1 %collective-permute-start = (bf16[32,8192]{1,0:T(8,128)(2,1)}, bf16[32,8192]{1,0:T(8,128)(2,1)S(1)}, u32[]{:S(2)}, u32[]{:S(2)}) collective-permute-start(bf16[32,8192]{1,0:T(8,128)(2,1)} %get-tuple-element.1128), channel_id=1, source_target_pairs={{0,32},{32,64},{64,96},{96,128},{128,160},{160,192},{192,224},{1,3... | collective-permute-start | bytes 1572872 | tf_op jit(solution)/shard_map/while/body/eval_jaxpr/ppermute | solution.py:13
  539.6 14.5 %collective-permute-start.1 = (bf16[32,8192]{1,0:T(8,128)(2,1)S(1)}, bf16[32,8192]{1,0:T(8,128)(2,1)S(1)}, u32[]{:S(2)}, u32[]{:S(2)}) collective-permute-start(bf16[32,8192]{1,0:T(8,128)(2,1)S(1)} %get-tuple-element.1156), channel_id=1, source_target_pairs={{32,0},{64,32},{96,64},{128,96},{160,128},{192,160},{224,192},{33,... | collective-permute-start | bytes 1572872 | tf_op jit(solution)/shard_map/while/body/eval_jaxpr/ppermute | solution.py:13
  558.4 20.8 %collective-permute-start.1 = (bf16[32,8192]{1,0:T(8,128)(2,1)S(1)}, bf16[32,8192]{1,0:T(8,128)(2,1)S(1)}, u32[]{:S(2)}, u32[]{:S(2)}) collective-permute-start(bf16[32,8192]{1,0:T(8,128)(2,1)S(1)} %get-tuple-element.1156), channel_id=1, source_target_pairs={{32,0},{64,32},{96,64},{128,96},{160,128},{192,160},{224,192},{33,... | collective-permute-start | bytes 1572872 | tf_op jit(solution)/shard_map/while/body/eval_jaxpr/ppermute | solution.py:13
  583.5 13.0 %collective-permute-start.1 = (bf16[32,8192]{1,0:T(8,128)(2,1)S(1)}, bf16[32,8192]{1,0:T(8,128)(2,1)S(1)}, u32[]{:S(2)}, u32[]{:S(2)}) collective-permute-start(bf16[32,8192]{1,0:T(8,128)(2,1)S(1)} %get-tuple-element.1156), channel_id=1, source_target_pairs={{32,0},{64,32},{96,64},{128,96},{160,128},{192,160},{224,192},{33,... | collective-permute-start | bytes 1572872 | tf_op jit(solution)/shard_map/while/body/eval_jaxpr/ppermute | solution.py:13
  600.8 23.4 %collective-permute-start.1 = (bf16[32,8192]{1,0:T(8,128)(2,1)S(1)}, bf16[32,8192]{1,0:T(8,128)(2,1)S(1)}, u32[]{:S(2)}, u32[]{:S(2)}) collective-permute-start(bf16[32,8192]{1,0:T(8,128)(2,1)S(1)} %get-tuple-element.1156), channel_id=1, source_target_pairs={{32,0},{64,32},{96,64},{128,96},{160,128},{192,160},{224,192},{33,... | collective-permute-start | bytes 1572872 | tf_op jit(solution)/shard_map/while/body/eval_jaxpr/ppermute | solution.py:13
  628.4 13.0 %collective-permute-start.1 = (bf16[32,8192]{1,0:T(8,128)(2,1)S(1)}, bf16[32,8192]{1,0:T(8,128)(2,1)S(1)}, u32[]{:S(2)}, u32[]{:S(2)}) collective-permute-start(bf16[32,8192]{1,0:T(8,128)(2,1)S(1)} %get-tuple-element.1156), channel_id=1, source_target_pairs={{32,0},{64,32},{96,64},{128,96},{160,128},{192,160},{224,192},{33,... | collective-permute-start | bytes 1572872 | tf_op jit(solution)/shard_map/while/body/eval_jaxpr/ppermute | solution.py:13
  645.6 20.8 %collective-permute-start.1 = (bf16[32,8192]{1,0:T(8,128)(2,1)S(1)}, bf16[32,8192]{1,0:T(8,128)(2,1)S(1)}, u32[]{:S(2)}, u32[]{:S(2)}) collective-permute-start(bf16[32,8192]{1,0:T(8,128)(2,1)S(1)} %get-tuple-element.1156), channel_id=1, source_target_pairs={{32,0},{64,32},{96,64},{128,96},{160,128},{192,160},{224,192},{33,... | collective-permute-start | bytes 1572872 | tf_op jit(solution)/shard_map/while/body/eval_jaxpr/ppermute | solution.py:13
  670.7 115.2 %collective-permute-start.1 = (bf16[32,8192]{1,0:T(8,128)(2,1)S(1)}, bf16[32,8192]{1,0:T(8,128)(2,1)S(1)}, u32[]{:S(2)}, u32[]{:S(2)}) collective-permute-start(bf16[32,8192]{1,0:T(8,128)(2,1)S(1)} %get-tuple-element.1156), channel_id=1, source_target_pairs={{32,0},{64,32},{96,64},{128,96},{160,128},{192,160},{224,192},{33,... | collective-permute-start | bytes 1572872 | tf_op jit(solution)/shard_map/while/body/eval_jaxpr/ppermute | solution.py:13
  868.5 12.3 collective-permute-start.1
  912.3 322.1 %reduce-scatter.2.cloned.1.call-start = ((), (), s32[]{:S(2)}) async-start(), calls=%async_computation.1 | async-start | bytes 1081344 | tf_op jit(solution)/shard_map/reduce_scatter | solution.py:236
  (18 other events, 379.2 us)
Sparse Core Ops, SparseCore 0:
  10.4 68.8 all-gather.8
  81.2 72.0 all-gather.6
  155.0 89.4 all-gather.10
  912.4 206.9 all-reduce.1
  1121.9 112.4 reduce-scatter.1
where the time goes:
time: 1250 us; the launch traced here: 1240 us
  waiting for transfers between devices  821 us (66%)
  other arithmetic  151 us (12%)
  starting transfers between devices  123 us (10%)
  matrix products  107 us (9%)
  local copies, waits for them, and re-layouts  26 us (2%)
  between operations  13.8 us (1%)
    ppermute x22, waiting for transfers between devices, shifted(): lax.ppermute(value, axis, [(source, source + steps) for source in range(i...  269 us
    psum x1, waiting for transfers between devices, per_device(): lax.psum(state_done[2].astype(jnp.bfloat16), 'dp').astype(jnp.float32)  204 us
    ppermute x22, starting transfers between devices, shifted(): lax.ppermute(value, axis, [(source, source + steps) for source in range(i...  122 us
    reduce_scatter x1, waiting for transfers between devices, per_device(): lax.psum_scatter(state_done[1].astype(jnp.bfloat16), 'dp', scatter_dimens...  113 us
    all_gather x1, waiting for transfers between devices, per_device(): out_full = lax.all_gather(output_projection[0], 'dp', axis=1, tiled=True)  91.3 us
    all_gather x1, waiting for transfers between devices, per_device(): lax.all_gather(value_projection[0], 'dp', axis=0, tiled=True)  73.9 us
    all_gather x1, waiting for transfers between devices, per_device(): lax.all_gather(adapter_down_factor[0], 'dp', axis=0, tiled=True)  68.3 us
    add x22, other arithmetic, backward_step(): return (outgoing, total_down + down_factor_term, total_up + up_factor_term)  33.3 us
  transfers between devices with their start and end apart: 27, of which 27 were waited for; matrix products, arithmetic and copies ran while one was open for 6% of the time, Pallas kernels for 0%

commit v1 on v0

v1 whole, which is shorter than its diff:
```python
import functools

import jax
import jax.numpy as jnp
from jax import lax
from jax.experimental import pallas as pl
from jax.experimental.pallas import tpu as pltpu
from jax.sharding import PartitionSpec as P

ADAPTER_SCALE = 2.0
NORM_EPS = 1e-05
NX = 4
MESH = pl.DeviceIdType.MESH
F32 = jnp.float32
BF16 = jnp.bfloat16


def dot_nn(a, b):
    return lax.dot_general(a, b, (((1,), (0,)), ((), ())), preferred_element_type=F32)


def dot_nt(a, b):
    return lax.dot_general(a, b, (((1,), (1,)), ((), ())), preferred_element_type=F32)


def dot_tn(a, b):
    return lax.dot_general(a, b, (((0,), (0,)), ((), ())), preferred_element_type=F32)


def two_parts(value):
    high = value.astype(BF16)
    low = (value - high.astype(F32)).astype(BF16)
    return high, low


def kernel(
    cfg,
    h_ref,
    o_ref,
    v_ref,
    a_ref,
    b_ref,
    g_ref,
    lg_ref,
    sw_ref,
    cg_ref,
    gd_ref,
    gu_ref,
    weights,
    states,
    grad,
    part,
    arrived,
    spread,
    totals,
    up_sums,
    scal,
    grad_out,
    grad_in,
    up_part,
    up_z,
    up_q,
    own_send,
    relay_send,
    core_send,
    weight_recv,
    h_send,
    h_recv,
    part_send,
    part_recv,
    spread_send,
    spread_recv,
    scal_send,
    scal_recv,
    grad_send,
    grad_recv,
    up_send,
    up_recv,
):
    NSEC, NZ, TOK, FB, VW, RANK, WIDTH, CANDLEN = cfg
    NY = NSEC // 2
    SLAB = 4 * FB
    ROWS = NZ * TOK
    UPR = RANK // 4
    QW = VW // FB
    R_V, R_A = VW, 2 * VW
    R_B = R_A + RANK
    R_G = R_B + UPR * QW
    R_END = R_G + 16
    SPLIT = (R_END // 32) * 16
    halves = (pl.ds(0, SPLIT), pl.ds(SPLIT, R_END - SPLIT))
    PW = VW + 128
    GROWS = RANK + UPR * QW

    sec = lax.axis_index("section")
    dp = lax.axis_index("dp")
    y, x_hi = sec // 2, sec % 2
    z, quarter = dp // 4, dp % 4
    x_lo, core = quarter // 2, quarter % 2
    x = x_hi * 2 + x_lo

    def device(xx, yy, zz, cc):
        return {"section": yy * 2 + xx // 2, "dp": zz * 4 + (xx % 2) * 2 + cc}

    def z_peer(d):
        zz = lax.rem(z + d, NZ)
        return zz, {"section": sec, "dp": zz * 4 + quarter}

    def place(xx, yy, cc):
        return yy * 2 + xx // 2, (xx % 2) * 2 + cc

    barrier = pltpu.get_barrier_semaphore()
    my_slot = sec * 4 + quarter

    def greet(slot, carry):
        @pl.when(slot != my_slot)
        def _():
            pl.semaphore_signal(
                barrier,
                inc=1,
                device_id={"section": slot // 4, "dp": z * 4 + slot % 4},
                device_id_type=MESH,
            )

        return carry

    lax.fori_loop(0, NSEC * 4, greet, 0)
    for d in range(1, NZ):
        pl.semaphore_signal(barrier, inc=1, device_id=z_peer(d)[1], device_id_type=MESH)
    pl.semaphore_wait(barrier, NSEC * 4 - 1 + NZ - 1)

    g_own = g_ref[:, pl.ds(pl.multiple_of(dp * FB, FB), FB)]
    g1, g1r = g_own.astype(BF16), g_own
    g_rest = g1r - g1.astype(F32)
    g2 = g_rest.astype(BF16)
    g3 = (g_rest - g2.astype(F32)).astype(BF16)
    row_id = lax.broadcasted_iota(jnp.int32, (16, FB), 0)
    g_rows = jnp.where(
        row_id == 0,
        g1.astype(F32),
        jnp.where(row_id == 1, g2.astype(F32), jnp.where(row_id == 2, g3.astype(F32), 0.0)),
    ).astype(BF16)
    weights[sec, quarter, 0:VW] = o_ref[...]
    weights[sec, quarter, R_V:R_A] = v_ref[...].T
    weights[sec, quarter, R_A:R_B] = a_ref[...].T
    up_rows = b_ref[pl.ds(pl.multiple_of(quarter * UPR, UPR), UPR), :]
    for w in range(QW):
        weights[sec, quarter, R_B + w * UPR : R_B + (w + 1) * UPR] = up_rows[
            :, w * FB : (w + 1) * FB
        ]
    weights[sec, quarter, R_G:R_END] = g_rows

    def weight_copy(xx, yy, half, target, send_sem):
        k, q = place(xx, yy, core)
        return pltpu.make_async_remote_copy(
            src_ref=weights.at[k, q, halves[half]],
            dst_ref=weights.at[k, q, halves[half]],
            send_sem=send_sem,
            recv_sem=weight_recv.at[k * 4 + q, half],
            device_id=target,
            device_id_type=MESH,
        )

    tok_row = pl.multiple_of(sec * TOK, TOK)

    def h_copy(d):
        zz, target = z_peer(d)
        return pltpu.make_async_remote_copy(
            src_ref=h_ref.at[pl.ds(tok_row, TOK), pl.ds(pl.multiple_of(zz * SLAB, SLAB), SLAB)],
            dst_ref=states.at[0, z],
            send_sem=h_send.at[d],
            recv_sem=h_recv.at[z],
            device_id=target,
            device_id_type=MESH,
        )

    sends = []
    own_states = pltpu.make_async_copy(
        h_ref.at[pl.ds(tok_row, TOK), pl.ds(pl.multiple_of(z * SLAB, SLAB), SLAB)],
        states.at[0, z],
        h_send.at[0],
    )
    own_states.start()
    for d in range(1, NZ):
        copy = h_copy(d)
        copy.start()
        sends.append(copy)

    for half in (0, 1):
        for i in range(1, NX):
            copy = weight_copy(
                x, y, half, device(lax.rem(x + i, NX), y, z, core), own_send.at[0, i, half]
            )
            copy.start()
            sends.append(copy)
        for j in range(1, NY):
            copy = weight_copy(
                x, y, 1 - half, device(x, lax.rem(y + j, NY), z, core), own_send.at[1, j, 1 - half]
            )
            copy.start()
            sends.append(copy)

    def weight_wait(k, q, rows, half):
        pltpu.make_async_copy(
            weights.at[k, q, rows], weights.at[k, q, rows], weight_recv.at[k * 4 + q, half]
        ).wait()

    for i in range(1, max(NX, NY)):
        if i < NX:
            xs = lax.rem(x + i, NX)
            k, q = place(xs, y, core)
            weight_wait(k, q, halves[0], 0)
            for j in range(1, NY):
                copy = weight_copy(
                    xs, y, 0, device(x, lax.rem(y + j, NY), z, core), relay_send.at[0, i, j]
                )
                copy.start()
                sends.append(copy)
        if i < NY:
            ys = lax.rem(y + i, NY)
            k, q = place(x, ys, core)
            weight_wait(k, q, halves[1], 1)
            for j in range(1, NX):
                copy = weight_copy(
                    x, ys, 1, device(lax.rem(x + j, NX), y, z, core), relay_send.at[1, i, j]
                )
                copy.start()
                sends.append(copy)

    whole = pl.ds(0, R_END)

    def core_copy(layer, lo):
        q = lo * 2 + core
        return pltpu.make_async_remote_copy(
            src_ref=weights.at[layer, q],
            dst_ref=weights.at[layer, q],
            send_sem=core_send.at[layer, lo],
            recv_sem=weight_recv.at[layer * 4 + q, 0],
            device_id=device(x, y, z, 1 - core),
            device_id_type=MESH,
        )

    def pass_on(layer):
        xs_hi, ys = layer % 2, layer // 2
        for lo in (0, 1):
            xs = xs_hi * 2 + lo
            q = lo * 2 + core

            @pl.when(ys != y)
            def _():
                weight_wait(layer, q, halves[0], 0)

            @pl.when(xs != x)
            def _():
                weight_wait(layer, q, halves[1], 1)

            core_copy(layer, lo).start()

    def take_over(layer):
        for lo in (0, 1):
            weight_wait(layer, lo * 2 + (1 - core), whole, 0)

    def gains(layer, q):
        return jnp.sum(weights[layer, q, R_G:R_END].astype(F32), axis=0, keepdims=True)

    def ups(layer):
        return [
            jnp.concatenate(
                [weights[layer, q, R_B + w * UPR : R_B + (w + 1) * UPR] for q in range(4)], axis=0
            )
            for w in range(QW)
        ]

    def part_copy(step, d):
        zz, target = z_peer(d)
        return pltpu.make_async_remote_copy(
            src_ref=part.at[zz],
            dst_ref=arrived.at[step, z],
            send_sem=part_send.at[d],
            recv_sem=part_recv.at[z],
            device_id=target,
            device_id_type=MESH,
        )

    def part_wait(step, d):
        zz = lax.rem(z + d, NZ)
        pltpu.make_async_copy(
            arrived.at[step, zz], arrived.at[step, zz], part_recv.at[zz]
        ).wait()

    def spread_copy(step, d):
        zz, target = z_peer(d)
        return pltpu.make_async_remote_copy(
            src_ref=spread.at[step, z],
            dst_ref=spread.at[step, z],
            send_sem=spread_send.at[d],
            recv_sem=spread_recv.at[z],
            device_id=target,
            device_id_type=MESH,
        )

    def spread_wait(step, d):
        zz = lax.rem(z + d, NZ)
        pltpu.make_async_copy(
            spread.at[step, zz], spread.at[step, zz], spread_recv.at[zz]
        ).wait()

    def exchange_start(step):
        for d in range(1, NZ):
            part_copy(step, d).start()

    def exchange_sum(step):
        for d in range(1, NZ):
            part_wait(step, d)
        total = part[z].astype(F32)
        for d in range(1, NZ):
            total = total + arrived[step, lax.rem(z + d, NZ)].astype(F32)
        return total

    def spread_all(step):
        for d in range(1, NZ):
            spread_copy(step, d).start()
        for d in range(1, NZ):
            part_copy(step, d).wait_send()
        for d in range(1, NZ):
            spread_wait(step, d)
        for d in range(1, NZ):
            spread_copy(step, d).wait_send()

    lane = lax.broadcasted_iota(jnp.int32, (ROWS, 128), 1)
    lane_own = lax.broadcasted_iota(jnp.int32, (TOK, 128), 1)

    def put_scalar(rank_part, scalar, lanes):
        high, low = two_parts(scalar)
        padded = jnp.concatenate([rank_part, jnp.zeros_like(rank_part)], axis=1)
        return jnp.where(
            lanes == RANK,
            high.astype(F32),
            jnp.where(lanes == RANK + 1, low.astype(F32), padded),
        )

    def get_scalar(tile, lanes):
        return jnp.sum(jnp.where(lanes >= RANK, tile, 0.0), axis=1, keepdims=True)

    pass_on(jnp.int32(0))
    own_states.wait()
    for d in range(1, NZ):
        zz = lax.rem(z + d, NZ)
        pltpu.make_async_copy(states.at[0, zz], states.at[0, zz], h_recv.at[zz]).wait()

    def forward_step(layer, carry):
        take_over(layer)
        ss = jnp.zeros((ROWS, 1), F32)
        value = jnp.zeros((ROWS, VW + RANK), F32)
        for q in range(4):
            xq = states[layer, :, :, q * FB : (q + 1) * FB].reshape(ROWS, FB).astype(F32)
            ss = ss + jnp.sum(xq * xq, axis=1, keepdims=True)
            xg = (xq * gains(layer, q)).astype(BF16)
            value = value + dot_nt(xg, weights[layer, q, R_V:R_B])
        part[:, :, 0:VW] = value[:, 0:VW].astype(BF16).reshape(NZ, TOK, VW)
        part[:, :, VW:PW] = (
            put_scalar(value[:, VW:], ss, lane).astype(BF16).reshape(NZ, TOK, 128)
        )
        exchange_start(layer)

        @pl.when(layer + 1 < NSEC)
        def _():
            pass_on(layer + 1)

        total = exchange_sum(layer)
        totals[layer] = total
        tail = total[:, VW:PW]
        r = lax.rsqrt(get_scalar(tail, lane_own) / WIDTH + NORM_EPS)
        t = (r * tail[:, 0:RANK]).astype(BF16)
        for w, up in enumerate(ups(layer)):
            cols = slice(w * FB, (w + 1) * FB)
            spread[layer, z, :, cols] = (
                r * total[:, cols] + ADAPTER_SCALE * dot_nn(t, up)
            ).astype(BF16)
        spread_all(layer)
        v = spread[layer, :, :, 0:VW].reshape(ROWS, VW)
        for q in range(4):
            cols = slice(q * FB, (q + 1) * FB)
            xq = states[layer, :, :, cols].reshape(ROWS, FB).astype(F32)
            states[layer + 1, :, :, cols] = (
                (xq + dot_nn(v, weights[layer, q, 0:VW])).astype(BF16).reshape(NZ, TOK, FB)
            )
        return carry

    lax.fori_loop(0, NSEC, forward_step, 0)

    slab = pl.ds(pl.multiple_of(z * SLAB, SLAB), SLAB)
    head = lg_ref[:, slab] * sw_ref[:, slab]
    last = states[NSEC].reshape(ROWS, SLAB).astype(F32)
    ss = jnp.sum(last * last, axis=1, keepdims=True)
    inner = jnp.sum(last * head, axis=1, keepdims=True)
    rows = lax.broadcasted_iota(jnp.int32, (ROWS, 128), 0)
    mine = jnp.logical_and(rows >= z * TOK, rows < (z + 1) * TOK)
    token_grad = jnp.where(mine, cg_ref[sec * TOK // CANDLEN, 0], 0.0)
    table = jnp.where(
        lane == 0, ss, jnp.where(lane == 1, inner, jnp.where(lane == 2, token_grad, 0.0))
    )
    scal[z] = table.T[0:8]

    def scal_copy(d):
        zz, target = z_peer(d)
        return pltpu.make_async_remote_copy(
            src_ref=scal.at[z],
            dst_ref=scal.at[z],
            send_sem=scal_send.at[d],
            recv_sem=scal_recv.at[z],
            device_id=target,
            device_id_type=MESH,
        )

    for d in range(1, NZ):
        copy = scal_copy(d)
        copy.start()
        sends.append(copy)
    for d in range(1, NZ):
        zz = lax.rem(z + d, NZ)
        pltpu.make_async_copy(scal.at[zz], scal.at[zz], scal_recv.at[zz]).wait()
    table = jnp.concatenate([jnp.sum(scal[...], axis=0)] * 16, axis=0).T
    if ROWS != 128:
        table = table[0:ROWS]
    ss = jnp.sum(jnp.where(lane == 0, table, 0.0), axis=1, keepdims=True)
    inner = jnp.sum(jnp.where(lane == 1, table, 0.0), axis=1, keepdims=True)
    token_grad = jnp.sum(jnp.where(lane == 2, table, 0.0), axis=1, keepdims=True)
    factor = lax.rsqrt(ss / WIDTH + NORM_EPS)
    token_grad = token_grad / CANDLEN
    grad[...] = (
        token_grad * factor * head
        - token_grad * factor * factor * factor * inner / WIDTH * last
    ).astype(BF16)

    def grad_copy(layer, q):
        return pltpu.make_async_remote_copy(
            src_ref=grad_out.at[layer, q],
            dst_ref=grad_in.at[my_slot],
            send_sem=grad_send.at[layer, q],
            recv_sem=grad_recv.at[my_slot],
            device_id={"section": layer, "dp": z * 4 + q},
            device_id_type=MESH,
        )

    def backward_step(index, carry):
        layer = NSEC - 1 - index
        step = NSEC + index
        value = jnp.zeros((ROWS, VW), F32)
        for q in range(4):
            value = value + dot_nt(grad[:, q * FB : (q + 1) * FB], weights[layer, q, 0:VW])
        part[:, :, 0:VW] = value.astype(BF16).reshape(NZ, TOK, VW)
        exchange_start(step)
        forward_total = totals[layer]
        tail = forward_total[:, VW:PW]
        r = lax.rsqrt(get_scalar(tail, lane_own) / WIDTH + NORM_EPS)
        t = (r * tail[:, 0:RANK]).astype(BF16)
        dv32 = exchange_sum(step)[:, 0:VW]
        dv = dv32.astype(BF16)
        dt32 = jnp.zeros((TOK, RANK), F32)
        for w, up in enumerate(ups(layer)):
            dt32 = dt32 + dot_nt(dv[:, w * FB : (w + 1) * FB], up)
        dt = (ADAPTER_SCALE * dt32).astype(BF16)
        dvf, dtf = dv.astype(F32), dt.astype(F32)
        inner = jnp.sum(dvf * forward_total[:, 0:VW], axis=1, keepdims=True) + jnp.sum(
            dtf * tail[:, 0:RANK], axis=1, keepdims=True
        )
        shrink = r * r * r * inner / WIDTH
        spread[step, z, :, 0:VW] = (r * dvf).astype(BF16)
        spread[step, z, :, VW:PW] = put_scalar(r * dtf, shrink, lane_own).astype(BF16)
        up_sums[...] = ADAPTER_SCALE * dot_tn(t, dv)
        spread_all(step)
        both = spread[step].reshape(ROWS, PW)
        scaled = both[:, 0 : VW + RANK]
        rdt = both[:, VW : VW + RANK]
        shrink = get_scalar(both[:, VW:PW].astype(F32), lane)
        for q in range(4):
            cols = slice(q * FB, (q + 1) * FB)
            xq = states[layer, :, :, cols].reshape(ROWS, FB)
            gq = gains(layer, q)
            grad_out[layer, q, 0:RANK] = (dot_tn(rdt, xq) * gq).astype(BF16)
            for w in range(QW):
                grad_out[layer, q, RANK + w * UPR : RANK + (w + 1) * UPR] = up_sums[
                    q * UPR : (q + 1) * UPR, w * FB : (w + 1) * FB
                ].astype(BF16)

            here = jnp.logical_and(layer == sec, quarter == q)

            @pl.when(jnp.logical_not(here))
            def _():
                grad_copy(layer, q).start()

            @pl.when(here)
            def _():
                grad_in[my_slot] = grad_out[layer, q]

        @pl.when(layer > 0)
        def _():
            for q in range(4):
                cols = slice(q * FB, (q + 1) * FB)
                xq = states[layer, :, :, cols].reshape(ROWS, FB).astype(F32)
                du = dot_nn(scaled, weights[layer, q, R_V:R_B])
                grad[:, cols] = (
                    grad[:, cols].astype(F32) + du * gains(layer, q) - shrink * xq
                ).astype(BF16)

        return carry

    lax.fori_loop(0, NSEC, backward_step, 0)

    def collect(slot, carry):
        @pl.when(slot != my_slot)
        def _():
            pltpu.make_async_copy(grad_in.at[slot], grad_in.at[slot], grad_recv.at[slot]).wait()

        return carry

    lax.fori_loop(0, NSEC * 4, collect, 0)
    summed = jnp.sum(grad_in[...].astype(F32), axis=0)
    up_z[z] = summed[RANK:GROWS].astype(BF16)
    for d in range(1, NZ):
        zz, target = z_peer(d)
        copy = pltpu.make_async_remote_copy(
            src_ref=up_z.at[z],
            dst_ref=up_z.at[z],
            send_sem=up_send.at[0, d],
            recv_sem=up_recv.at[0, z],
            device_id=target,
            device_id_type=MESH,
        )
        copy.start()
        sends.append(copy)
    gd_ref[...] = summed[0:RANK].T
    for d in range(1, NZ):
        zz = lax.rem(z + d, NZ)
        pltpu.make_async_copy(up_z.at[zz], up_z.at[zz], up_recv.at[0, zz]).wait()
    up_q[quarter] = jnp.sum(up_z[...].astype(F32), axis=0)
    for d in range(1, 4):
        copy = pltpu.make_async_remote_copy(
            src_ref=up_q.at[quarter],
            dst_ref=up_q.at[quarter],
            send_sem=up_send.at[1, d],
            recv_sem=up_recv.at[1, quarter],
            device_id={"section": sec, "dp": z * 4 + lax.rem(quarter + d, 4)},
            device_id_type=MESH,
        )
        copy.start()
        sends.append(copy)
    for d in range(1, 4):
        qq = lax.rem(quarter + d, 4)
        pltpu.make_async_copy(up_q.at[qq], up_q.at[qq], up_recv.at[1, qq]).wait()
    for q in range(4):
        for w in range(QW):
            gu_ref[q * UPR : (q + 1) * UPR, w * FB : (w + 1) * FB] = up_q[
                q, w * UPR : (w + 1) * UPR
            ]

    for copy in sends:
        copy.wait_send()

    def drain(layer, carry):
        for lo in (0, 1):
            core_copy(layer, lo).wait_send()
        for q in range(4):

            @pl.when(jnp.logical_not(jnp.logical_and(layer == sec, quarter == q)))
            def _():
                grad_copy(layer, q).wait_send()

        return carry

    lax.fori_loop(0, NSEC, drain, 0)


def per_device(
    block_hidden_input,
    cached_score_gradient,
    value_projection,
    output_projection,
    adapter_down_factor,
    adapter_up_factor,
    input_norm_gain,
    last_norm_gain,
    scoring_head_weight,
):
    nsec = lax.axis_size("section")
    nz = lax.axis_size("dp") // 4
    blocks, cand_len, width = block_hidden_input.shape
    tok = blocks * cand_len // nsec
    fb, vw = value_projection.shape[1:]
    rank = adapter_down_factor.shape[2]
    slab, rows = 4 * fb, nz * tok
    upr, qw = rank // 4, vw // fb
    r_end = 2 * vw + rank + upr * qw + 16
    pw = vw + 128
    grows = rank + upr * qw
    cfg = (nsec, nz, tok, fb, vw, rank, width, cand_len)
    vmem = pl.BlockSpec(memory_space=pltpu.VMEM)
    dma = pltpu.SemaphoreType.DMA
    grad_down, grad_up = pl.pallas_call(
        functools.partial(kernel, cfg),
        out_shape=(
            jax.ShapeDtypeStruct((fb, rank), F32),
            jax.ShapeDtypeStruct((rank, vw), F32),
        ),
        in_specs=[pl.BlockSpec(memory_space=pl.ANY)]
        + [vmem] * 7
        + [pl.BlockSpec(memory_space=pltpu.SMEM)],
        out_specs=(vmem, vmem),
        scratch_shapes=[
            pltpu.VMEM((nsec, 4, r_end, fb), BF16),
            pltpu.VMEM((nsec + 1, nz, tok, slab), BF16),
            pltpu.VMEM((rows, slab), BF16),
            pltpu.VMEM((nz, tok, pw), BF16),
            pltpu.VMEM((2 * nsec, nz, tok, pw), BF16),
            pltpu.VMEM((2 * nsec, nz, tok, pw), BF16),
            pltpu.VMEM((nsec, tok, pw), F32),
            pltpu.VMEM((rank, vw), F32),
            pltpu.VMEM((nz, 8, 128), F32),
            pltpu.VMEM((nsec, 4, grows, fb), BF16),
            pltpu.VMEM((nsec * 4, grows, fb), BF16),
            pltpu.VMEM((upr * qw, fb), F32),
            pltpu.VMEM((nz, upr * qw, fb), BF16),
            pltpu.VMEM((4, upr * qw, fb), F32),
            dma((2, 4, 2)),
            dma((2, 4, 4)),
            dma((nsec, 2)),
            dma((nsec * 4, 2)),
            dma((nz,)),
            dma((nz,)),
            dma((nz,)),
            dma((nz,)),
            dma((nz,)),
            dma((nz,)),
            dma((nz,)),
            dma((nz,)),
            dma((nsec, 4)),
            dma((nsec * 4,)),
            dma((2, 8)),
            dma((2, 8)),
        ],
        compiler_params=pltpu.CompilerParams(
            collective_id=0, has_side_effects=True, vmem_limit_bytes=56 * 1024 * 1024
        ),
        name="layers",
    )(
        block_hidden_input.reshape(blocks * cand_len, width),
        output_projection[0],
        value_projection[0],
        adapter_down_factor[0],
        adapter_up_factor[0],
        input_norm_gain,
        last_norm_gain.reshape(1, width),
        scoring_head_weight.reshape(1, width),
        cached_score_gradient,
    )
    return (grad_down[None], grad_up[None])


def solution(mesh):
    return jax.shard_map(
        per_device,
        mesh=mesh,
        in_specs=(
            P(None, "dp", None),
            P(None, "dp"),
            P("section", "dp", None),
            P("section", None, "dp"),
            P("section", "dp", None),
            P("section", None, None),
            P("section", None),
            P(),
            P(),
        ),
        out_specs=(P("section", "dp", None), P("section", None, None)),
        check_vma=False,
    )
```

time: 1250 us -> 345 us (0.28)
  waiting for transfers between devices: 821 us -> 0 us
  Pallas kernels: 0 us -> 338 us
  other arithmetic: 151 us -> 0 us
  starting transfers between devices: 123 us -> 0 us
  matrix products: 107 us -> 0 us
  local copies, waits for them, and re-layouts: 26 us -> 5.99 us
  between operations: 13.8 us -> 0.64 us
    pallas_call x0 -> x1, Pallas kernels: none -> 338 us  [per_device(): pl.pallas_call(functools.partial(kernel, cfg), out_shape=(jax.ShapeDtypeS...]
    ppermute x22 -> x0, waiting for transfers between devices: 269 us -> none  [shifted(): lax.ppermute(value, axis, [(source, source + steps) for source in range(i...]
    all_gather x3 -> x0, waiting for transfers between devices: 233 us -> none  [the longest x1 91.3 us: per_device(): out_full = lax.all_gather(output_projection[0], 'dp', axis=1, tiled=True)]
    psum x1 -> x0, waiting for transfers between devices: 204 us -> none  [per_device(): lax.psum(state_done[2].astype(jnp.bfloat16), 'dp').astype(jnp.float32)]
    ppermute x22 -> x0, starting transfers between devices: 122 us -> none  [shifted(): lax.ppermute(value, axis, [(source, source + steps) for source in range(i...]
    reduce_scatter x1 -> x0, waiting for transfers between devices: 113 us -> none  [per_device(): lax.psum_scatter(state_done[1].astype(jnp.bfloat16), 'dp', scatter_dimens...]
    dot_general x36 -> x0, matrix products: 107 us -> none  [the longest x4 24.4 us: layer_backward_pass(): jnp.einsum('rd,kd->rk', following_gradient, output_projection, preferred_...]
    select_n x33 -> x0, other arithmetic: 65.7 us -> none  [the longest x11 26.9 us: forward_step(): jnp.where(active, lax.dynamic_update_index_in_dim(carried[3], normalized_...]
  transfers between devices with their start and end apart: 27 -> 0, of which waited for: 27 -> 0; matrix products, arithmetic and copies ran while one was open for 6% -> 0% of each run, Pallas kernels for 0% -> 0%
where the time goes in v1:
time: 345 us
  Pallas kernels  338 us (98%)
  local copies, waits for them, and re-layouts  5.99 us (2%)
    pallas_call x1, Pallas kernels, per_device(): pl.pallas_call(functools.partial(kernel, cfg), out_shape=(jax.ShapeDtypeS...  338 us

profile of v1, /device:TPU:1, one launch (start us, length us, event | category | flops | bytes accessed | tf_op | source)
XLA Modules:
  0.0 345.1 jit_solution(14211314478353552343)
XLA Ops:
  0.6 1.3 copy.12.cg_ref
  1.9 1.5 copy.11
  3.4 338.5 %layers.1 = (f32[256,64]{1,0:T(8,128)}, f32[64,512]{1,0:T(8,128)}) custom-call(bf16[128,8192]{1,0:T(8,128)(2,1)} %bitcast.9, bf16[512,256]{1,0:T(8,128)(2,1)} %bitcast.10, bf16[256,512]{1,0:T(8,128)(2,1)} %bitcast.11, bf16[256,64]{1,0:T(8,128)(2,1)} %bitcast.12, bf16[64,512]{1,0:T(8,128)(2,1)} %bitcast.15, f32[1,8192]{1,0:T(1,128)} %g_ref.1, ...), custom_call_target="tpu_custom_call" | custom-call | tf_op jit(solution)/shard_map/layers/pallas_call | solution.py:600
  341.9 1.6 copy.13
  343.5 1.6 copy.15

commit v2 on v1

--- a/solution.py
+++ b/solution.py
@@ -53,11 +53,10 @@
     arrived,
     spread,
     totals,
-    up_sums,
+    down_sums,
     scal,
     grad_out,
     grad_in,
-    up_part,
     up_z,
     up_q,
     own_send,
@@ -162,70 +161,109 @@
         )
 
     tok_row = pl.multiple_of(sec * TOK, TOK)
-
-    def h_copy(d):
+    HALF = NZ // 2
+    SR = HALF * TOK
+    stream, owner = z % 2, z // 2
+    my_rows = stream * HALF + owner
+
+    def slot_of(zz):
+        return (zz % 2) * HALF + zz // 2
+
+    sends = []
+    own_states = pltpu.make_async_copy(
+        h_ref.at[pl.ds(tok_row, TOK), pl.ds(pl.multiple_of(z * SLAB, SLAB), SLAB)],
+        states.at[0, my_rows],
+        h_send.at[0],
+    )
+    own_states.start()
+    for d in range(1, NZ):
         zz, target = z_peer(d)
-        return pltpu.make_async_remote_copy(
+        copy = pltpu.make_async_remote_copy(
             src_ref=h_ref.at[pl.ds(tok_row, TOK), pl.ds(pl.multiple_of(zz * SLAB, SLAB), SLAB)],
-            dst_ref=states.at[0, z],
+            dst_ref=states.at[0, my_rows],
             send_sem=h_send.at[d],
             recv_sem=h_recv.at[z],
             device_id=target,
             device_id_type=MESH,
         )
-
-    sends = []
-    own_states = pltpu.make_async_copy(
-        h_ref.at[pl.ds(tok_row, TOK), pl.ds(pl.multiple_of(z * SLAB, SLAB), SLAB)],
-        states.at[0, z],
-        h_send.at[0],
-    )
-    own_states.start()
-    for d in range(1, NZ):
-        copy = h_copy(d)
         copy.start()
         sends.append(copy)
-
-    for half in (0, 1):
-        for i in range(1, NX):
-            copy = weight_copy(
-                x, y, half, device(lax.rem(x + i, NX), y, z, core), own_send.at[0, i, half]
-            )
-            copy.start()
-            sends.append(copy)
-        for j in range(1, NY):
-            copy = weight_copy(
-                x, y, 1 - half, device(x, lax.rem(y + j, NY), z, core), own_send.at[1, j, 1 - half]
-            )
-            copy.start()
-            sends.append(copy)
 
     def weight_wait(k, q, rows, half):
         pltpu.make_async_copy(
             weights.at[k, q, rows], weights.at[k, q, rows], weight_recv.at[k * 4 + q, half]
         ).wait()
 
-    for i in range(1, max(NX, NY)):
-        if i < NX:
-            xs = lax.rem(x + i, NX)
-            k, q = place(xs, y, core)
+    def after(i, n):
+        return lax.rem(i + 1, n)
+
+    def before(i, n):
+        return lax.rem(i + n - 1, n)
+
+    y_next, y_prev, x_next, x_prev = after(y, NY), before(y, NY), after(x, NX), before(x, NX)
+
+    def column_copies():
+        up, down = device(x, y_next, z, core), device(x, y_prev, z, core)
+        return [
+            weight_copy(x, y, half, target, own_send.at[i])
+            for i, (half, target) in enumerate(((0, up), (1, down), (1, up), (0, down)))
+        ]
+
+    def column_relays():
+        return [
+            weight_copy(x, y_prev, 0, device(x, y_next, z, core), own_send.at[4]),
+            weight_copy(x, y_next, 1, device(x, y_prev, z, core), own_send.at[5]),
+        ]
+
+    def row_copies(ys):
+        right, left = device(x_next, y, z, core), device(x_prev, y, z, core)
+        return [
+            weight_copy(x, ys, half, target, relay_send.at[ys, i])
+            for i, (half, target) in enumerate(((0, right), (1, left), (1, right), (0, left)))
+        ]
+
+    def row_relays(ys):
+        return [
+            weight_copy(x_prev, ys, 0, device(x_next, y, z, core), relay_send.at[ys, 4]),
+            weight_copy(x_next, ys, 1, device(x_prev, y, z, core), relay_send.at[ys, 5]),
+        ]
+
+    def row_send(ys):
+        k, q = place(x, ys, core)
+
+        @pl.when(jnp.logical_and(ys != y, ys != y_prev))
+        def _():
             weight_wait(k, q, halves[0], 0)
-            for j in range(1, NY):
-                copy = weight_copy(
-                    xs, y, 0, device(x, lax.rem(y + j, NY), z, core), relay_send.at[0, i, j]
-                )
-                copy.start()
-                sends.append(copy)
-        if i < NY:
-            ys = lax.rem(y + i, NY)
-            k, q = place(x, ys, core)
+
+        @pl.when(jnp.logical_and(ys != y, ys != y_next))
+        def _():
             weight_wait(k, q, halves[1], 1)
-            for j in range(1, NX):
-                copy = weight_copy(
-                    x, ys, 1, device(lax.rem(x + j, NX), y, z, core), relay_send.at[1, i, j]
-                )
-                copy.start()
-                sends.append(copy)
+
+        for copy in row_copies(ys):
+            copy.start()
+
+    def row_relay(ys):
+        first, second = row_relays(ys)
+        k, q = place(x_prev, ys, core)
+        weight_wait(k, q, halves[0], 0)
+        first.start()
+        k, q = place(x_next, ys, core)
+        weight_wait(k, q, halves[1], 1)
+        second.start()
+
+    if NY > 1:
+        for copy in column_copies():
+            copy.start()
+        first, second = column_relays()
+        k, q = place(x, y_prev, core)
+        weight_wait(k, q, halves[0], 0)
+        first.start()
+        k, q = place(x, y_next, core)
+        weight_wait(k, q, halves[1], 1)
+        second.start()
+    for ys in range(NY):
+        row_send(ys)
+    row_relay(0)
 
     whole = pl.ds(0, R_END)
 
@@ -241,16 +279,15 @@
         )
 
     def pass_on(layer):
-        xs_hi, ys = layer % 2, layer // 2
         for lo in (0, 1):
-            xs = xs_hi * 2 + lo
+            xs = (layer % 2) * 2 + lo
             q = lo * 2 + core
 
-            @pl.when(ys != y)
+            @pl.when(jnp.logical_and(xs != x, xs != x_prev))
             def _():
                 weight_wait(layer, q, halves[0], 0)
 
-            @pl.when(xs != x)
+            @pl.when(jnp.logical_and(xs != x, xs != x_next))
             def _():
                 weight_wait(layer, q, halves[1], 1)
 
@@ -271,62 +308,80 @@
             for w in range(QW)
         ]
 
-    def part_copy(step, d):
-        zz, target = z_peer(d)
+    def peer(st, d):
+        zz = 2 * lax.rem(owner + d, HALF) + st
+        return zz, {"section": sec, "dp": zz * 4 + quarter}
+
+    def part_copy(st, step, d, lanes):
+        zz, target = peer(st, d)
         return pltpu.make_async_remote_copy(
-            src_ref=part.at[zz],
-            dst_ref=arrived.at[step, z],
-            send_sem=part_send.at[d],
+            src_ref=part.at[st, zz // 2, :, pl.ds(0, lanes)],
+            dst_ref=arrived.at[step, z, :, pl.ds(0, lanes)],
+            send_sem=part_send.at[st, d],
             recv_sem=part_recv.at[z],
             device_id=target,
             device_id_type=MESH,
         )
 
-    def part_wait(step, d):
-        zz = lax.rem(z + d, NZ)
-        pltpu.make_async_copy(
-            arrived.at[step, zz], arrived.at[step, zz], part_recv.at[zz]
-        ).wait()
-
-    def spread_copy(step, d):
-        zz, target = z_peer(d)
+    def spread_copy(step, d, lanes):
+        target = z_peer(d)[1]
         return pltpu.make_async_remote_copy(
-            src_ref=spread.at[step, z],
-            dst_ref=spread.at[step, z],
+            src_ref=spread.at[step, my_rows, :, pl.ds(0, lanes)],
+            dst_ref=spread.at[step, my_rows, :, pl.ds(0, lanes)],
             send_sem=spread_send.at[d],
             recv_sem=spread_recv.at[z],
             device_id=target,
             device_id_type=MESH,
         )
 
-    def spread_wait(step, d):
-        zz = lax.rem(z + d, NZ)
-        pltpu.make_async_copy(
-            spread.at[step, zz], spread.at[step, zz], spread_recv.at[zz]
-        ).wait()
-
-    def exchange_start(step):
+    def exchange_start(st, step, lanes):
+        @pl.when(stream != st)
+        def _():
+            part_copy(st, step, 0, lanes).start()
+
+        for d in range(1, HALF):
+            part_copy(st, step, d, lanes).start()
+
+    def exchange_sum(st, step, lanes):
         for d in range(1, NZ):
-            part_copy(step, d).start()
-
-    def exchange_sum(step):
+            zz = lax.rem(z + d, NZ)
+            ref = arrived.at[step, zz, :, pl.ds(0, lanes)]
+            pltpu.make_async_copy(ref, ref, part_recv.at[zz]).wait()
+        total = part[st, owner, :, 0:lanes].astype(F32)
         for d in range(1, NZ):
-            part_wait(step, d)
-        total = part[z].astype(F32)
+            total = total + arrived[step, lax.rem(z + d, NZ), :, 0:lanes].astype(F32)
+        return total
+
+    def spread_start(step, lanes):
         for d in range(1, NZ):
-            total = total + arrived[step, lax.rem(z + d, NZ)].astype(F32)
-        return total
-
-    def spread_all(step):
-        for d in range(1, NZ):
-            spread_copy(step, d).start()
-        for d in range(1, NZ):
-            part_copy(step, d).wait_send()
-        for d in range(1, NZ):
-            spread_wait(step, d)
-        for d in range(1, NZ):
-            spread_copy(step, d).wait_send()
-
+            spread_copy(step, d, lanes).start()
+
+    def exchange_end(st, step, part_lanes, lanes):
+        @pl.when(stream != st)
+        def _():
+            part_copy(st, step, 0, part_lanes).wait_send()
+
+        for d in range(1, HALF):
+            part_copy(st, step, d, part_lanes).wait_send()
+
+        def arrive(d):
+            zz = peer(st, d)[0]
+            ref = spread.at[step, slot_of(zz), :, pl.ds(0, lanes)]
+            pltpu.make_async_copy(ref, ref, spread_recv.at[zz]).wait()
+
+        @pl.when(stream != st)
+        def _():
+            arrive(0)
+
+        for d in range(1, HALF):
+            arrive(d)
+
+        @pl.when(stream == st)
+        def _():
+            for d in range(1, NZ):
+                spread_copy(step, d, lanes).wait_send()
+
+    lane_stream = lax.broadcasted_iota(jnp.int32, (SR, 128), 1)
     lane = lax.broadcasted_iota(jnp.int32, (ROWS, 128), 1)
     lane_own = lax.broadcasted_iota(jnp.int32, (TOK, 128), 1)
 
@@ -346,48 +401,84 @@
     own_states.wait()
     for d in range(1, NZ):
         zz = lax.rem(z + d, NZ)
-        pltpu.make_async_copy(states.at[0, zz], states.at[0, zz], h_recv.at[zz]).wait()
-
-    def forward_step(layer, carry):
-        take_over(layer)
-        ss = jnp.zeros((ROWS, 1), F32)
-        value = jnp.zeros((ROWS, VW + RANK), F32)
+        ref = states.at[0, slot_of(zz)]
+        pltpu.make_async_copy(ref, ref, h_recv.at[zz]).wait()
+
+    def rows_of(layer, st, q):
+        own_rows = slice(st * HALF, (st + 1) * HALF)
+        return states[layer, own_rows, :, q * FB : (q + 1) * FB].reshape(SR, FB)
+
+    def forward_part(st, layer):
+        ss = jnp.zeros((SR, 1), F32)
+        value = jnp.zeros((SR, VW + RANK), F32)
         for q in range(4):
-            xq = states[layer, :, :, q * FB : (q + 1) * FB].reshape(ROWS, FB).astype(F32)
+            xq = rows_of(layer, st, q).astype(F32)
             ss = ss + jnp.sum(xq * xq, axis=1, keepdims=True)
             xg = (xq * gains(layer, q)).astype(BF16)
             value = value + dot_nt(xg, weights[layer, q, R_V:R_B])
-        part[:, :, 0:VW] = value[:, 0:VW].astype(BF16).reshape(NZ, TOK, VW)
-        part[:, :, VW:PW] = (
-            put_scalar(value[:, VW:], ss, lane).astype(BF16).reshape(NZ, TOK, 128)
-        )
-        exchange_start(layer)
+        part[st, :, :, 0:VW] = value[:, 0:VW].astype(BF16).reshape(HALF, TOK, VW)
+        part[st, :, :, VW:PW] = (
+            put_scalar(value[:, VW:], ss, lane_stream).astype(BF16).reshape(HALF, TOK, 128)
+        )
+        exchange_start(st, layer, PW)
+
+    def forward_own(st, layer):
+        @pl.when(stream == st)
+        def _():
+            total = exchange_sum(st, layer, PW)
+            totals[layer] = total
+            tail = total[:, VW:PW]
+            r = lax.rsqrt(get_scalar(tail, lane_own) / WIDTH + NORM_EPS)
+            t = (r * tail[:, 0:RANK]).astype(BF16)
+            for w, up in enumerate(ups(layer)):
+                cols = slice(w * FB, (w + 1) * FB)
+                spread[layer, my_rows, :, cols] = (
+                    r * total[:, cols] + ADAPTER_SCALE * dot_nn(t, up)
+                ).astype(BF16)
+            spread_start(layer, VW)
+
+    def forward_end(st, layer):
+        exchange_end(st, layer, PW, VW)
+        own_rows = slice(st * HALF, (st + 1) * HALF)
+        v = spread[layer, own_rows, :, 0:VW].reshape(SR, VW)
+        for q in range(4):
+            xq = rows_of(layer, st, q).astype(F32)
+            states[layer + 1, own_rows, :, q * FB : (q + 1) * FB] = (
+                (xq + dot_nn(v, weights[layer, q, 0:VW])).astype(BF16).reshape(HALF, TOK, FB)
+            )
+
+    take_over(jnp.int32(0))
+    forward_part(0, jnp.int32(0))
+
+    def forward_step(layer, carry):
+        @pl.when(layer > 0)
+        def _():
+            forward_end(1, layer - 1)
+
+        forward_part(1, layer)
+
+        @pl.when(jnp.logical_and(layer % 2 == 0, layer // 2 + 1 < NY))
+        def _():
+            row_relay(layer // 2 + 1)
+
+        forward_own(0, layer)
+        forward_own(1, layer)
 
         @pl.when(layer + 1 < NSEC)
         def _():
             pass_on(layer + 1)
 
-        total = exchange_sum(layer)
-        totals[layer] = total
-        tail = total[:, VW:PW]
-        r = lax.rsqrt(get_scalar(tail, lane_own) / WIDTH + NORM_EPS)
-        t = (r * tail[:, 0:RANK]).astype(BF16)
-        for w, up in enumerate(ups(layer)):
-            cols = slice(w * FB, (w + 1) * FB)
-            spread[layer, z, :, cols] = (
-                r * total[:, cols] + ADAPTER_SCALE * dot_nn(t, up)
-            ).astype(BF16)
-        spread_all(layer)
-        v = spread[layer, :, :, 0:VW].reshape(ROWS, VW)
-        for q in range(4):
-            cols = slice(q * FB, (q + 1) * FB)
-            xq = states[layer, :, :, cols].reshape(ROWS, FB).astype(F32)
-            states[layer + 1, :, :, cols] = (
-                (xq + dot_nn(v, weights[layer, q, 0:VW])).astype(BF16).reshape(NZ, TOK, FB)
-            )
+        forward_end(0, layer)
+
+        @pl.when(layer + 1 < NSEC)
+        def _():
+            take_over(layer + 1)
+            forward_part(0, layer + 1)
+
         return carry
 
     lax.fori_loop(0, NSEC, forward_step, 0)
+    forward_end(1, jnp.int32(NSEC - 1))
 
     slab = pl.ds(pl.multiple_of(z * SLAB, SLAB), SLAB)
     head = lg_ref[:, slab] * sw_ref[:, slab]
@@ -395,11 +486,13 @@
     ss = jnp.sum(last * last, axis=1, keepdims=True)
     inner = jnp.sum(last * head, axis=1, keepdims=True)
     rows = lax.broadcasted_iota(jnp.int32, (ROWS, 128), 0)
-    mine = jnp.logical_and(rows >= z * TOK, rows < (z + 1) * TOK)
+    mine = jnp.logical_and(rows >= my_rows * TOK, rows < (my_rows + 1) * TOK)
     token_grad = jnp.where(mine, cg_ref[sec * TOK // CANDLEN, 0], 0.0)
     table = jnp.where(
         lane == 0, ss, jnp.where(lane == 1, inner, jnp.where(lane == 2, token_grad, 0.0))
     )
+    if ROWS != 128:
+        table = jnp.concatenate([table] * (128 // ROWS), axis=0)
     scal[z] = table.T[0:8]
 
     def scal_copy(d):
@@ -443,47 +536,72 @@
             device_id_type=MESH,
         )
 
-    def backward_step(index, carry):
-        layer = NSEC - 1 - index
-        step = NSEC + index
-        value = jnp.zeros((ROWS, VW), F32)
+    def backward_part(st, layer):
+        value = jnp.zeros((SR, VW), F32)
         for q in range(4):
-            value = value + dot_nt(grad[:, q * FB : (q + 1) * FB], weights[layer, q, 0:VW])
-        part[:, :, 0:VW] = value.astype(BF16).reshape(NZ, TOK, VW)
-        exchange_start(step)
-        forward_total = totals[layer]
-        tail = forward_total[:, VW:PW]
-        r = lax.rsqrt(get_scalar(tail, lane_own) / WIDTH + NORM_EPS)
-        t = (r * tail[:, 0:RANK]).astype(BF16)
-        dv32 = exchange_sum(step)[:, 0:VW]
-        dv = dv32.astype(BF16)
-        dt32 = jnp.zeros((TOK, RANK), F32)
-        for w, up in enumerate(ups(layer)):
-            dt32 = dt32 + dot_nt(dv[:, w * FB : (w + 1) * FB], up)
-        dt = (ADAPTER_SCALE * dt32).astype(BF16)
-        dvf, dtf = dv.astype(F32), dt.astype(F32)
-        inner = jnp.sum(dvf * forward_total[:, 0:VW], axis=1, keepdims=True) + jnp.sum(
-            dtf * tail[:, 0:RANK], axis=1, keepdims=True
-        )
-        shrink = r * r * r * inner / WIDTH
-        spread[step, z, :, 0:VW] = (r * dvf).astype(BF16)
-        spread[step, z, :, VW:PW] = put_scalar(r * dtf, shrink, lane_own).astype(BF16)
-        up_sums[...] = ADAPTER_SCALE * dot_tn(t, dv)
-        spread_all(step)
-        both = spread[step].reshape(ROWS, PW)
+            value = value + dot_nt(
+                grad[st * SR : (st + 1) * SR, q * FB : (q + 1) * FB], weights[layer, q, 0:VW]
+            )
+        part[st, :, :, 0:VW] = value.astype(BF16).reshape(HALF, TOK, VW)
+        exchange_start(st, 2 * NSEC - 1 - layer, VW)
+
+    def backward_own(st, layer):
+        step = 2 * NSEC - 1 - layer
+
+        @pl.when(stream == st)
+        def _():
+            forward_total = totals[layer]
+            tail = forward_total[:, VW:PW]
+            r = lax.rsqrt(get_scalar(tail, lane_own) / WIDTH + NORM_EPS)
+            t = (r * tail[:, 0:RANK]).astype(BF16)
+            dv = exchange_sum(st, step, VW).astype(BF16)
+            dt32 = jnp.zeros((TOK, RANK), F32)
+            for w, up in enumerate(ups(layer)):
+                dt32 = dt32 + dot_nt(dv[:, w * FB : (w + 1) * FB], up)
+            dt = (ADAPTER_SCALE * dt32).astype(BF16)
+            dvf, dtf = dv.astype(F32), dt.astype(F32)
+            inner = jnp.sum(dvf * forward_total[:, 0:VW], axis=1, keepdims=True) + jnp.sum(
+                dtf * tail[:, 0:RANK], axis=1, keepdims=True
+            )
+            shrink = r * r * r * inner / WIDTH
+            spread[step, my_rows, :, 0:VW] = (r * dvf).astype(BF16)
+            spread[step, my_rows, :, VW:PW] = put_scalar(r * dtf, shrink, lane_own).astype(BF16)
+            spread_start(step, PW)
+            up_sum = (ADAPTER_SCALE * dot_tn(t, dv)).astype(BF16)
+            for q in range(4):
+                for w in range(QW):
+                    grad_out[layer, q, RANK + w * UPR : RANK + (w + 1) * UPR] = up_sum[
+                        q * UPR : (q + 1) * UPR, w * FB : (w + 1) * FB
+                    ]
+
+    def backward_end(st, layer):
+        step = 2 * NSEC - 1 - layer
+        exchange_end(st, step, VW, PW)
+        both = spread[step, st * HALF : (st + 1) * HALF].reshape(SR, PW)
         scaled = both[:, 0 : VW + RANK]
-        rdt = both[:, VW : VW + RANK]
-        shrink = get_scalar(both[:, VW:PW].astype(F32), lane)
+        shrink = get_scalar(both[:, VW:PW].astype(F32), lane_stream)
+        own_rows = slice(st * SR, (st + 1) * SR)
+
+        @pl.when(layer > 0)
+        def _():
+            for q in range(4):
+                cols = slice(q * FB, (q + 1) * FB)
+                du = dot_nn(scaled, weights[layer, q, R_V:R_B])
+                grad[own_rows, cols] = (
+                    grad[own_rows, cols].astype(F32)
+                    + du * gains(layer, q)
+                    - shrink * rows_of(layer, st, q).astype(F32)
+                ).astype(BF16)
+
+    def backward_sums(st, layer):
+        step = 2 * NSEC - 1 - layer
+        rdt = spread[step, st * HALF : (st + 1) * HALF, :, VW : VW + RANK].reshape(SR, RANK)
         for q in range(4):
-            cols = slice(q * FB, (q + 1) * FB)
-            xq = states[layer, :, :, cols].reshape(ROWS, FB)
-            gq = gains(layer, q)
-            grad_out[layer, q, 0:RANK] = (dot_tn(rdt, xq) * gq).astype(BF16)
-            for w in range(QW):
-                grad_out[layer, q, RANK + w * UPR : RANK + (w + 1) * UPR] = up_sums[
-                    q * UPR : (q + 1) * UPR, w * FB : (w + 1) * FB
-                ].astype(BF16)
-
+            share = dot_tn(rdt, rows_of(layer, st, q)) * gains(layer, q)
+            if st == 0:
+                down_sums[q] = share
+                continue
+            grad_out[layer, q, 0:RANK] = (down_sums[q] + share).astype(BF16)
             here = jnp.logical_and(layer == sec, quarter == q)
 
             @pl.when(jnp.logical_not(here))
@@ -494,19 +612,35 @@
             def _():
                 grad_in[my_slot] = grad_out[layer, q]
 
+    backward_part(0, jnp.int32(NSEC - 1))
+
+    def backward_step(index, carry):
+        layer = NSEC - 1 - index
+
+        @pl.when(index > 0)
+        def _():
+            backward_end(1, layer + 1)
+
+        backward_part(1, layer)
+
+        @pl.when(index > 0)
+        def _():
+            backward_sums(1, layer + 1)
+
+        backward_own(0, layer)
+        backward_own(1, layer)
+        backward_end(0, layer)
+
         @pl.when(layer > 0)
         def _():
-            for q in range(4):
-                cols = slice(q * FB, (q + 1) * FB)
-                xq = states[layer, :, :, cols].reshape(ROWS, FB).astype(F32)
-                du = dot_nn(scaled, weights[layer, q, R_V:R_B])
-                grad[:, cols] = (
-                    grad[:, cols].astype(F32) + du * gains(layer, q) - shrink * xq
-                ).astype(BF16)
-
+            backward_part(0, layer - 1)
+
+        backward_sums(0, layer)
         return carry
 
     lax.fori_loop(0, NSEC, backward_step, 0)
+    backward_end(1, jnp.int32(0))
+    backward_sums(1, jnp.int32(0))
 
     def collect(slot, carry):
         @pl.when(slot != my_slot)
@@ -557,6 +691,12 @@
 
     for copy in sends:
         copy.wait_send()
+    if NY > 1:
+        for copy in column_copies() + column_relays():
+            copy.wait_send()
+    for ys in range(NY):
+        for copy in row_copies(ys) + row_relays(ys):
+            copy.wait_send()
 
     def drain(layer, carry):
         for lo in (0, 1):
@@ -611,24 +751,23 @@
             pltpu.VMEM((nsec, 4, r_end, fb), BF16),
             pltpu.VMEM((nsec + 1, nz, tok, slab), BF16),
             pltpu.VMEM((rows, slab), BF16),
-            pltpu.VMEM((nz, tok, pw), BF16),
+            pltpu.VMEM((2, nz // 2, tok, pw), BF16),
             pltpu.VMEM((2 * nsec, nz, tok, pw), BF16),
             pltpu.VMEM((2 * nsec, nz, tok, pw), BF16),
             pltpu.VMEM((nsec, tok, pw), F32),
-            pltpu.VMEM((rank, vw), F32),
+            pltpu.VMEM((4, rank, fb), F32),
             pltpu.VMEM((nz, 8, 128), F32),
             pltpu.VMEM((nsec, 4, grows, fb), BF16),
             pltpu.VMEM((nsec * 4, grows, fb), BF16),
-            pltpu.VMEM((upr * qw, fb), F32),
             pltpu.VMEM((nz, upr * qw, fb), BF16),
             pltpu.VMEM((4, upr * qw, fb), F32),
-            dma((2, 4, 2)),
-            dma((2, 4, 4)),
+            dma((6,)),
+            dma((nsec // 2, 6)),
             dma((nsec, 2)),
             dma((nsec * 4, 2)),
             dma((nz,)),
             dma((nz,)),
-            dma((nz,)),
+            dma((2, nz)),
             dma((nz,)),
             dma((nz,)),
             dma((nz,)),

time: 345 us -> 321 us (0.930)
  Pallas kernels: 338 us -> 314 us
    pallas_call x1, Pallas kernels: 338 us -> 314 us  [per_device(): pl.pallas_call(functools.partial(kernel, cfg), out_shape=(jax.ShapeDtypeS...]
where the time goes in v2:
time: 321 us; the launch traced here: 320 us
  Pallas kernels  314 us (98%)
  local copies, waits for them, and re-layouts  5.99 us (2%)
    pallas_call x1, Pallas kernels, per_device(): pl.pallas_call(functools.partial(kernel, cfg), out_shape=(jax.ShapeDtypeS...  314 us

profile of v2, /device:TPU:1, one launch (start us, length us, event | category | flops | bytes accessed | tf_op | source)
XLA Modules:
  0.0 320.5 jit_solution(17711864950219732924)
XLA Ops:
  0.6 1.3 copy.12.cg_ref
  1.9 1.5 copy.11
  3.4 313.9 %layers.1 = (f32[256,64]{1,0:T(8,128)}, f32[64,512]{1,0:T(8,128)}) custom-call(bf16[128,8192]{1,0:T(8,128)(2,1)} %bitcast.9, bf16[512,256]{1,0:T(8,128)(2,1)} %bitcast.10, bf16[256,512]{1,0:T(8,128)(2,1)} %bitcast.11, bf16[256,64]{1,0:T(8,128)(2,1)} %bitcast.12, bf16[64,512]{1,0:T(8,128)(2,1)} %bitcast.15, f32[1,8192]{1,0:T(1,128)} %g_ref.1, ...), custom_call_target="tpu_custom_call" | custom-call | tf_op jit(solution)/shard_map/layers/pallas_call | solution.py:740
  317.3 1.6 copy.13
  318.9 1.6 copy.15

commit v3 on v2

--- a/solution.py
+++ b/solution.py
@@ -85,9 +85,8 @@
     R_V, R_A = VW, 2 * VW
     R_B = R_A + RANK
     R_G = R_B + UPR * QW
-    R_END = R_G + 16
-    SPLIT = (R_END // 32) * 16
-    halves = (pl.ds(0, SPLIT), pl.ds(SPLIT, R_END - SPLIT))
+    R_END = -(-(R_G + 16) // 32) * 32
+    SPLIT = R_END // 2
     PW = VW + 128
     GROWS = RANK + UPR * QW
 
@@ -133,7 +132,7 @@
     g_rest = g1r - g1.astype(F32)
     g2 = g_rest.astype(BF16)
     g3 = (g_rest - g2.astype(F32)).astype(BF16)
-    row_id = lax.broadcasted_iota(jnp.int32, (16, FB), 0)
+    row_id = lax.broadcasted_iota(jnp.int32, (R_END - R_G, FB), 0)
     g_rows = jnp.where(
         row_id == 0,
         g1.astype(F32),
@@ -141,7 +140,7 @@
     ).astype(BF16)
     weights[sec, quarter, 0:VW] = o_ref[...]
     weights[sec, quarter, R_V:R_A] = v_ref[...].T
-    weights[sec, quarter, R_A:R_B] = a_ref[...].T
+    weights[sec, quarter, R_A:R_B] = a_ref[...]
     up_rows = b_ref[pl.ds(pl.multiple_of(quarter * UPR, UPR), UPR), :]
     for w in range(QW):
         weights[sec, quarter, R_B + w * UPR : R_B + (w + 1) * UPR] = up_rows[
@@ -149,11 +148,14 @@
         ]
     weights[sec, quarter, R_G:R_END] = g_rows
 
+    def rows_half(half):
+        return pl.ds(pl.multiple_of(half * SPLIT, 16), SPLIT)
+
     def weight_copy(xx, yy, half, target, send_sem):
         k, q = place(xx, yy, core)
         return pltpu.make_async_remote_copy(
-            src_ref=weights.at[k, q, halves[half]],
-            dst_ref=weights.at[k, q, halves[half]],
+            src_ref=weights.at[k, q, rows_half(half)],
+            dst_ref=weights.at[k, q, rows_half(half)],
             send_sem=send_sem,
             recv_sem=weight_recv.at[k * 4 + q, half],
             device_id=target,
@@ -209,11 +211,9 @@
             for i, (half, target) in enumerate(((0, up), (1, down), (1, up), (0, down)))
         ]
 
-    def column_relays():
-        return [
-            weight_copy(x, y_prev, 0, device(x, y_next, z, core), own_send.at[4]),
-            weight_copy(x, y_next, 1, device(x, y_prev, z, core), own_send.at[5]),
-        ]
+    def column_relay(half):
+        source, target = (y_prev, y_next) if half == 0 else (y_next, y_prev)
+        return weight_copy(x, source, half, device(x, target, z, core), own_send.at[4 + half])
 
     def row_copies(ys):
         right, left = device(x_next, y, z, core), device(x_prev, y, z, core)
@@ -229,40 +229,52 @@
         ]
 
     def row_send(ys):
-        k, q = place(x, ys, core)
-
-        @pl.when(jnp.logical_and(ys != y, ys != y_prev))
-        def _():
-            weight_wait(k, q, halves[0], 0)
-
-        @pl.when(jnp.logical_and(ys != y, ys != y_next))
-        def _():
-            weight_wait(k, q, halves[1], 1)
-
         for copy in row_copies(ys):
             copy.start()
+
+    def column(ys, send_row):
+        k, q = place(x, ys, core)
+        first = jnp.where(y_next == ys, 1, 0)
+
+        @pl.when(y != ys)
+        def _():
+            for n in (0, 1):
+                half = first if n == 0 else 1 - first
+                weight_wait(k, q, rows_half(half), half)
+                if n == 0:
+
+                    @pl.when(y_prev == ys)
+                    def _():
+                        column_relay(0).start()
+
+                    @pl.when(y_next == ys)
+                    def _():
+                        column_relay(1).start()
+
+        if send_row:
+            row_send(ys)
 
     def row_relay(ys):
         first, second = row_relays(ys)
         k, q = place(x_prev, ys, core)
-        weight_wait(k, q, halves[0], 0)
+        weight_wait(k, q, rows_half(0), 0)
         first.start()
         k, q = place(x_next, ys, core)
-        weight_wait(k, q, halves[1], 1)
+        weight_wait(k, q, rows_half(1), 1)
         second.start()
 
-    if NY > 1:
+    @pl.when(jnp.logical_and(y == 0, NY > 1))
+    def _():
         for copy in column_copies():
             copy.start()
-        first, second = column_relays()
-        k, q = place(x, y_prev, core)
-        weight_wait(k, q, halves[0], 0)
-        first.start()
-        k, q = place(x, y_next, core)
-        weight_wait(k, q, halves[1], 1)
-        second.start()
-    for ys in range(NY):
-        row_send(ys)
+
+    column(0, True)
+
+    @pl.when(y != 0)
+    def _():
+        for copy in column_copies():
+            copy.start()
+
     row_relay(0)
 
     whole = pl.ds(0, R_END)
@@ -285,11 +297,11 @@
 
             @pl.when(jnp.logical_and(xs != x, xs != x_prev))
             def _():
-                weight_wait(layer, q, halves[0], 0)
+                weight_wait(layer, q, rows_half(0), 0)
 
             @pl.when(jnp.logical_and(xs != x, xs != x_next))
             def _():
-                weight_wait(layer, q, halves[1], 1)
+                weight_wait(layer, q, rows_half(1), 1)
 
             core_copy(layer, lo).start()
 
@@ -298,7 +310,7 @@
             weight_wait(layer, lo * 2 + (1 - core), whole, 0)
 
     def gains(layer, q):
-        return jnp.sum(weights[layer, q, R_G:R_END].astype(F32), axis=0, keepdims=True)
+        return jnp.sum(weights[layer, q, R_G : R_G + 16].astype(F32), axis=0, keepdims=True)
 
     def ups(layer):
         return [
@@ -398,6 +410,8 @@
         return jnp.sum(jnp.where(lanes >= RANK, tile, 0.0), axis=1, keepdims=True)
 
     pass_on(jnp.int32(0))
+    for ys in range(1, NY):
+        column(ys, ys == 1)
     own_states.wait()
     for d in range(1, NZ):
         zz = lax.rem(z + d, NZ)
@@ -457,12 +471,16 @@
 
         forward_part(1, layer)
 
-        @pl.when(jnp.logical_and(layer % 2 == 0, layer // 2 + 1 < NY))
-        def _():
-            row_relay(layer // 2 + 1)
+        @pl.when(jnp.logical_and(layer % 2 == 1, (layer + 3) // 2 < NY))
+        def _():
+            row_send((layer + 3) // 2)
 
         forward_own(0, layer)
         forward_own(1, layer)
+
+        @pl.when(jnp.logical_and(layer % 2 == 0, layer // 2 + 1 < NY))
+        def _():
+            row_relay(layer // 2 + 1)
 
         @pl.when(layer + 1 < NSEC)
         def _():
@@ -487,7 +505,7 @@
     inner = jnp.sum(last * head, axis=1, keepdims=True)
     rows = lax.broadcasted_iota(jnp.int32, (ROWS, 128), 0)
     mine = jnp.logical_and(rows >= my_rows * TOK, rows < (my_rows + 1) * TOK)
-    token_grad = jnp.where(mine, cg_ref[sec * TOK // CANDLEN, 0], 0.0)
+    token_grad = jnp.where(mine, cg_ref[0, sec * TOK // CANDLEN], 0.0)
     table = jnp.where(
         lane == 0, ss, jnp.where(lane == 1, inner, jnp.where(lane == 2, token_grad, 0.0))
     )
@@ -664,7 +682,7 @@
         )
         copy.start()
         sends.append(copy)
-    gd_ref[...] = summed[0:RANK].T
+    gd_ref[...] = summed[0:RANK]
     for d in range(1, NZ):
         zz = lax.rem(z + d, NZ)
         pltpu.make_async_copy(up_z.at[zz], up_z.at[zz], up_recv.at[0, zz]).wait()
@@ -692,7 +710,7 @@
     for copy in sends:
         copy.wait_send()
     if NY > 1:
-        for copy in column_copies() + column_relays():
+        for copy in column_copies() + [column_relay(0), column_relay(1)]:
             copy.wait_send()
     for ys in range(NY):
         for copy in row_copies(ys) + row_relays(ys):
@@ -731,7 +749,7 @@
     rank = adapter_down_factor.shape[2]
     slab, rows = 4 * fb, nz * tok
     upr, qw = rank // 4, vw // fb
-    r_end = 2 * vw + rank + upr * qw + 16
+    r_end = -(-(2 * vw + rank + upr * qw + 16) // 32) * 32
     pw = vw + 128
     grows = rank + upr * qw
     cfg = (nsec, nz, tok, fb, vw, rank, width, cand_len)
@@ -740,7 +758,7 @@
     grad_down, grad_up = pl.pallas_call(
         functools.partial(kernel, cfg),
         out_shape=(
-            jax.ShapeDtypeStruct((fb, rank), F32),
+            jax.ShapeDtypeStruct((rank, fb), F32),
             jax.ShapeDtypeStruct((rank, vw), F32),
         ),
         in_specs=[pl.BlockSpec(memory_space=pl.ANY)]
@@ -786,14 +804,14 @@
         block_hidden_input.reshape(blocks * cand_len, width),
         output_projection[0],
         value_projection[0],
-        adapter_down_factor[0],
+        adapter_down_factor[0].T,
         adapter_up_factor[0],
         input_norm_gain,
         last_norm_gain.reshape(1, width),
         scoring_head_weight.reshape(1, width),
-        cached_score_gradient,
+        cached_score_gradient.T,
     )
-    return (grad_down[None], grad_up[None])
+    return (grad_down.T[None], grad_up[None])
 
 
 def solution(mesh):

time: 321 us -> 297 us (0.925)
  Pallas kernels: 314 us -> 293 us
    pallas_call x1, Pallas kernels: 314 us -> 293 us  [per_device(): pl.pallas_call(functools.partial(kernel, cfg), out_shape=(jax.ShapeDtypeS...]
where the time goes in v3:
time: 297 us
  Pallas kernels  293 us (99%)
  local copies, waits for them, and re-layouts  3.04 us (1%)
    pallas_call x1, Pallas kernels, per_device(): pl.pallas_call(functools.partial(kernel, cfg), out_shape=(jax.ShapeDtypeS...  293 us

profile of v3, /device:TPU:1, one launch (start us, length us, event | category | flops | bytes accessed | tf_op | source)
XLA Modules:
  0.0 296.6 jit_solution(7620508902978691419)
XLA Ops:
  0.6 292.9 %layers.1 = (f32[64,256]{1,0:T(8,128)}, f32[64,512]{1,0:T(8,128)}) custom-call(bf16[128,8192]{1,0:T(8,128)(2,1)} %bitcast.14, bf16[512,256]{1,0:T(8,128)(2,1)} %bitcast.15, bf16[256,512]{1,0:T(8,128)(2,1)} %bitcast.16, bf16[64,256]{1,0:T(8,128)(2,1)} %bitcast.20, bf16[64,512]{1,0:T(8,128)(2,1)} %bitcast.18, f32[1,8192]{1,0:T(1,128)} %g_ref.1, ...), custom_call_target="tpu_custom_call" | custom-call | tf_op jit(solution)/shard_map/layers/pallas_call | solution.py:758
  293.5 1.5 copy.13
  295.0 1.6 copy.14

commit v4 on v3

--- a/solution.py
+++ b/solution.py
@@ -82,11 +82,10 @@
     ROWS = NZ * TOK
     UPR = RANK // 4
     QW = VW // FB
-    R_V, R_A = VW, 2 * VW
-    R_B = R_A + RANK
-    R_G = R_B + UPR * QW
-    R_END = -(-(R_G + 16) // 32) * 32
-    SPLIT = R_END // 2
+    R_V, R_A, R_G, R_O = 0, VW, VW + RANK, VW + RANK + 32
+    R_B = R_O + VW
+    R_END = R_B + UPR * QW
+    STARTS, SIZES = (0, R_O), (R_O // 2, (R_END - R_O) // 2)
     PW = VW + 128
     GROWS = RANK + UPR * QW
 
@@ -125,39 +124,40 @@
     lax.fori_loop(0, NSEC * 4, greet, 0)
     for d in range(1, NZ):
         pl.semaphore_signal(barrier, inc=1, device_id=z_peer(d)[1], device_id_type=MESH)
-    pl.semaphore_wait(barrier, NSEC * 4 - 1 + NZ - 1)
 
     g_own = g_ref[:, pl.ds(pl.multiple_of(dp * FB, FB), FB)]
     g1, g1r = g_own.astype(BF16), g_own
     g_rest = g1r - g1.astype(F32)
     g2 = g_rest.astype(BF16)
     g3 = (g_rest - g2.astype(F32)).astype(BF16)
-    row_id = lax.broadcasted_iota(jnp.int32, (R_END - R_G, FB), 0)
+    row_id = lax.broadcasted_iota(jnp.int32, (R_O - R_G, FB), 0)
     g_rows = jnp.where(
         row_id == 0,
         g1.astype(F32),
         jnp.where(row_id == 1, g2.astype(F32), jnp.where(row_id == 2, g3.astype(F32), 0.0)),
     ).astype(BF16)
-    weights[sec, quarter, 0:VW] = o_ref[...]
+    weights[sec, quarter, R_O:R_B] = o_ref[...]
     weights[sec, quarter, R_V:R_A] = v_ref[...].T
-    weights[sec, quarter, R_A:R_B] = a_ref[...]
+    weights[sec, quarter, R_A:R_G] = a_ref[...]
     up_rows = b_ref[pl.ds(pl.multiple_of(quarter * UPR, UPR), UPR), :]
     for w in range(QW):
         weights[sec, quarter, R_B + w * UPR : R_B + (w + 1) * UPR] = up_rows[
             :, w * FB : (w + 1) * FB
         ]
-    weights[sec, quarter, R_G:R_END] = g_rows
-
-    def rows_half(half):
-        return pl.ds(pl.multiple_of(half * SPLIT, 16), SPLIT)
-
-    def weight_copy(xx, yy, half, target, send_sem):
+    weights[sec, quarter, R_G:R_O] = g_rows
+
+    pl.semaphore_wait(barrier, NSEC * 4 - 1 + NZ - 1)
+
+    def rows_half(pt, half):
+        return pl.ds(pl.multiple_of(STARTS[pt] + half * SIZES[pt], 16), SIZES[pt])
+
+    def weight_copy(xx, yy, pt, half, target, send_sem):
         k, q = place(xx, yy, core)
         return pltpu.make_async_remote_copy(
-            src_ref=weights.at[k, q, rows_half(half)],
-            dst_ref=weights.at[k, q, rows_half(half)],
+            src_ref=weights.at[k, q, rows_half(pt, half)],
+            dst_ref=weights.at[k, q, rows_half(pt, half)],
             send_sem=send_sem,
-            recv_sem=weight_recv.at[k * 4 + q, half],
+            recv_sem=weight_recv.at[k * 4 + q, pt * 2 + half],
             device_id=target,
             device_id_type=MESH,
         )
@@ -191,10 +191,9 @@
         copy.start()
         sends.append(copy)
 
-    def weight_wait(k, q, rows, half):
-        pltpu.make_async_copy(
-            weights.at[k, q, rows], weights.at[k, q, rows], weight_recv.at[k * 4 + q, half]
-        ).wait()
+    def weight_wait(k, q, pt, half):
+        ref = weights.at[k, q, rows_half(pt, half)]
+        pltpu.make_async_copy(ref, ref, weight_recv.at[k * 4 + q, pt * 2 + half]).wait()
 
     def after(i, n):
         return lax.rem(i + 1, n)
@@ -204,110 +203,106 @@
 
     y_next, y_prev, x_next, x_prev = after(y, NY), before(y, NY), after(x, NX), before(x, NX)
 
-    def column_copies():
+    def column_copies(pt):
         up, down = device(x, y_next, z, core), device(x, y_prev, z, core)
         return [
-            weight_copy(x, y, half, target, own_send.at[i])
+            weight_copy(x, y, pt, half, target, own_send.at[pt, i])
             for i, (half, target) in enumerate(((0, up), (1, down), (1, up), (0, down)))
         ]
 
-    def column_relay(half):
+    def column_relay(pt, half):
         source, target = (y_prev, y_next) if half == 0 else (y_next, y_prev)
-        return weight_copy(x, source, half, device(x, target, z, core), own_send.at[4 + half])
-
-    def row_copies(ys):
+        target = device(x, target, z, core)
+        return weight_copy(x, source, pt, half, target, own_send.at[pt, 4 + half])
+
+    def row_copies(ys, pt):
         right, left = device(x_next, y, z, core), device(x_prev, y, z, core)
         return [
-            weight_copy(x, ys, half, target, relay_send.at[ys, i])
+            weight_copy(x, ys, pt, half, target, relay_send.at[ys * 2 + pt, i])
             for i, (half, target) in enumerate(((0, right), (1, left), (1, right), (0, left)))
         ]
 
-    def row_relays(ys):
-        return [
-            weight_copy(x_prev, ys, 0, device(x_next, y, z, core), relay_send.at[ys, 4]),
-            weight_copy(x_next, ys, 1, device(x_prev, y, z, core), relay_send.at[ys, 5]),
-        ]
-
-    def row_send(ys):
-        for copy in row_copies(ys):
+    def row_relay_copy(ys, pt, half):
+        source, target = (x_prev, x_next) if half == 0 else (x_next, x_prev)
+        target = device(target, y, z, core)
+        return weight_copy(source, ys, pt, half, target, relay_send.at[ys * 2 + pt, 4 + half])
+
+    def row_send(ys, pt):
+        for copy in row_copies(ys, pt):
             copy.start()
 
-    def column(ys, send_row):
+    def column(ys, pt):
         k, q = place(x, ys, core)
         first = jnp.where(y_next == ys, 1, 0)
 
         @pl.when(y != ys)
         def _():
-            for n in (0, 1):
-                half = first if n == 0 else 1 - first
-                weight_wait(k, q, rows_half(half), half)
-                if n == 0:
-
-                    @pl.when(y_prev == ys)
-                    def _():
-                        column_relay(0).start()
-
-                    @pl.when(y_next == ys)
-                    def _():
-                        column_relay(1).start()
-
-        if send_row:
-            row_send(ys)
-
-    def row_relay(ys):
-        first, second = row_relays(ys)
-        k, q = place(x_prev, ys, core)
-        weight_wait(k, q, rows_half(0), 0)
-        first.start()
-        k, q = place(x_next, ys, core)
-        weight_wait(k, q, rows_half(1), 1)
-        second.start()
-
-    @pl.when(jnp.logical_and(y == 0, NY > 1))
-    def _():
-        for copy in column_copies():
-            copy.start()
-
-    column(0, True)
-
-    @pl.when(y != 0)
-    def _():
-        for copy in column_copies():
-            copy.start()
-
-    row_relay(0)
-
-    whole = pl.ds(0, R_END)
-
-    def core_copy(layer, lo):
+            weight_wait(k, q, pt, first)
+
+            @pl.when(y_prev == ys)
+            def _():
+                column_relay(pt, 0).start()
+
+            @pl.when(y_next == ys)
+            def _():
+                column_relay(pt, 1).start()
+
+            weight_wait(k, q, pt, 1 - first)
+
+    def row_relay(ys, pt):
+        for half, source in ((0, x_prev), (1, x_next)):
+            k, q = place(source, ys, core)
+            weight_wait(k, q, pt, half)
+            row_relay_copy(ys, pt, half).start()
+
+    def core_copy(layer, lo, pt):
         q = lo * 2 + core
+        rows = pl.ds(STARTS[pt], 2 * SIZES[pt])
         return pltpu.make_async_remote_copy(
-            src_ref=weights.at[layer, q],
-            dst_ref=weights.at[layer, q],
-            send_sem=core_send.at[layer, lo],
-            recv_sem=weight_recv.at[layer * 4 + q, 0],
+            src_ref=weights.at[layer, q, rows],
+            dst_ref=weights.at[layer, q, rows],
+            send_sem=core_send.at[layer, lo * 2 + pt],
+            recv_sem=weight_recv.at[layer * 4 + q, pt * 2],
             device_id=device(x, y, z, 1 - core),
             device_id_type=MESH,
         )
 
-    def pass_on(layer):
+    def pass_on(layer, pt):
         for lo in (0, 1):
             xs = (layer % 2) * 2 + lo
             q = lo * 2 + core
 
             @pl.when(jnp.logical_and(xs != x, xs != x_prev))
             def _():
-                weight_wait(layer, q, rows_half(0), 0)
+                weight_wait(layer, q, pt, 0)
 
             @pl.when(jnp.logical_and(xs != x, xs != x_next))
             def _():
-                weight_wait(layer, q, rows_half(1), 1)
-
-            core_copy(layer, lo).start()
-
-    def take_over(layer):
+                weight_wait(layer, q, pt, 1)
+
+            core_copy(layer, lo, pt).start()
+
+    def take_over(layer, pt):
         for lo in (0, 1):
-            weight_wait(layer, lo * 2 + (1 - core), whole, 0)
+            q = lo * 2 + (1 - core)
+            ref = weights.at[layer, q, pl.ds(STARTS[pt], 2 * SIZES[pt])]
+            pltpu.make_async_copy(ref, ref, weight_recv.at[layer * 4 + q, pt * 2]).wait()
+
+    @pl.when(jnp.logical_and(y == 0, NY > 1))
+    def _():
+        for copy in column_copies(0) + column_copies(1):
+            copy.start()
+
+    for pt in (0, 1):
+        column(0, pt)
+        row_send(0, pt)
+
+    @pl.when(y != 0)
+    def _():
+        for copy in column_copies(0) + column_copies(1):
+            copy.start()
+
+    row_relay(0, 0)
 
     def gains(layer, q):
         return jnp.sum(weights[layer, q, R_G : R_G + 16].astype(F32), axis=0, keepdims=True)
@@ -346,13 +341,16 @@
             device_id_type=MESH,
         )
 
+    far_first = sorted(range(1, NZ), key=lambda d: -min(d, NZ - d))
+    owners_far_first = sorted(range(1, HALF), key=lambda d: -min(d, HALF - d))
+
     def exchange_start(st, step, lanes):
+        for d in owners_far_first:
+            part_copy(st, step, d, lanes).start()
+
         @pl.when(stream != st)
         def _():
             part_copy(st, step, 0, lanes).start()
-
-        for d in range(1, HALF):
-            part_copy(st, step, d, lanes).start()
 
     def exchange_sum(st, step, lanes):
         for d in range(1, NZ):
@@ -365,7 +363,7 @@
         return total
 
     def spread_start(step, lanes):
-        for d in range(1, NZ):
+        for d in far_first:
             spread_copy(step, d, lanes).start()
 
     def exchange_end(st, step, part_lanes, lanes):
@@ -394,7 +392,6 @@
                 spread_copy(step, d, lanes).wait_send()
 
     lane_stream = lax.broadcasted_iota(jnp.int32, (SR, 128), 1)
-    lane = lax.broadcasted_iota(jnp.int32, (ROWS, 128), 1)
     lane_own = lax.broadcasted_iota(jnp.int32, (TOK, 128), 1)
 
     def put_scalar(rank_part, scalar, lanes):
@@ -409,9 +406,7 @@
     def get_scalar(tile, lanes):
         return jnp.sum(jnp.where(lanes >= RANK, tile, 0.0), axis=1, keepdims=True)
 
-    pass_on(jnp.int32(0))
-    for ys in range(1, NY):
-        column(ys, ys == 1)
+    pass_on(jnp.int32(0), 0)
     own_states.wait()
     for d in range(1, NZ):
         zz = lax.rem(z + d, NZ)
@@ -429,7 +424,7 @@
             xq = rows_of(layer, st, q).astype(F32)
             ss = ss + jnp.sum(xq * xq, axis=1, keepdims=True)
             xg = (xq * gains(layer, q)).astype(BF16)
-            value = value + dot_nt(xg, weights[layer, q, R_V:R_B])
+            value = value + dot_nt(xg, weights[layer, q, R_V:R_G])
         part[st, :, :, 0:VW] = value[:, 0:VW].astype(BF16).reshape(HALF, TOK, VW)
         part[st, :, :, VW:PW] = (
             put_scalar(value[:, VW:], ss, lane_stream).astype(BF16).reshape(HALF, TOK, 128)
@@ -439,12 +434,13 @@
     def forward_own(st, layer):
         @pl.when(stream == st)
         def _():
+            up_factor = ups(layer)
             total = exchange_sum(st, layer, PW)
             totals[layer] = total
             tail = total[:, VW:PW]
             r = lax.rsqrt(get_scalar(tail, lane_own) / WIDTH + NORM_EPS)
             t = (r * tail[:, 0:RANK]).astype(BF16)
-            for w, up in enumerate(ups(layer)):
+            for w, up in enumerate(up_factor):
                 cols = slice(w * FB, (w + 1) * FB)
                 spread[layer, my_rows, :, cols] = (
                     r * total[:, cols] + ADAPTER_SCALE * dot_nn(t, up)
@@ -458,11 +454,17 @@
         for q in range(4):
             xq = rows_of(layer, st, q).astype(F32)
             states[layer + 1, own_rows, :, q * FB : (q + 1) * FB] = (
-                (xq + dot_nn(v, weights[layer, q, 0:VW])).astype(BF16).reshape(HALF, TOK, FB)
+                (xq + dot_nn(v, weights[layer, q, R_O:R_B])).astype(BF16).reshape(HALF, TOK, FB)
             )
 
-    take_over(jnp.int32(0))
+    take_over(jnp.int32(0), 0)
     forward_part(0, jnp.int32(0))
+    row_relay(0, 1)
+    for ys in range(1, NY):
+        for pt in (0, 1):
+            column(ys, pt)
+            if ys == 1:
+                row_send(ys, pt)
 
     def forward_step(layer, carry):
         @pl.when(layer > 0)
@@ -471,94 +473,123 @@
 
         forward_part(1, layer)
 
+        pass_on(layer, 1)
+
         @pl.when(jnp.logical_and(layer % 2 == 1, (layer + 3) // 2 < NY))
         def _():
-            row_send((layer + 3) // 2)
-
+            for pt in (0, 1):
+                row_send((layer + 3) // 2, pt)
+
+        take_over(layer, 1)
         forward_own(0, layer)
         forward_own(1, layer)
 
         @pl.when(jnp.logical_and(layer % 2 == 0, layer // 2 + 1 < NY))
         def _():
-            row_relay(layer // 2 + 1)
+            for pt in (0, 1):
+                row_relay(layer // 2 + 1, pt)
 
         @pl.when(layer + 1 < NSEC)
         def _():
-            pass_on(layer + 1)
+            pass_on(layer + 1, 0)
 
         forward_end(0, layer)
 
         @pl.when(layer + 1 < NSEC)
         def _():
-            take_over(layer + 1)
+            take_over(layer + 1, 0)
             forward_part(0, layer + 1)
 
         return carry
 
+    slab = pl.ds(pl.multiple_of(z * SLAB, SLAB), SLAB)
+
+    def scal_copy(st, d):
+        return pltpu.make_async_remote_copy(
+            src_ref=scal.at[st, z],
+            dst_ref=scal.at[st, z],
+            send_sem=scal_send.at[st, d],
+            recv_sem=scal_recv.at[st, z],
+            device_id=z_peer(d)[1],
+            device_id_type=MESH,
+        )
+
+    def last_rows(st):
+        rows = states[NSEC, st * HALF : (st + 1) * HALF]
+        return rows.reshape(SR, SLAB).astype(F32), lg_ref[:, slab] * sw_ref[:, slab]
+
+    def seed_start(st):
+        last, head = last_rows(st)
+        ss = jnp.sum(last * last, axis=1, keepdims=True)
+        inner = jnp.sum(last * head, axis=1, keepdims=True)
+        rows = lax.broadcasted_iota(jnp.int32, (SR, 128), 0)
+        mine = jnp.logical_and(
+            stream == st, jnp.logical_and(rows >= owner * TOK, rows < (owner + 1) * TOK)
+        )
+        token_grad = jnp.where(mine, cg_ref[0, sec * TOK // CANDLEN], 0.0)
+        table = jnp.where(
+            lane_stream == 0,
+            ss,
+            jnp.where(lane_stream == 1, inner, jnp.where(lane_stream == 2, token_grad, 0.0)),
+        )
+        scal[st, z] = jnp.concatenate([table] * (128 // SR), axis=0).T[0:8]
+        for d in far_first:
+            copy = scal_copy(st, d)
+            copy.start()
+            sends.append(copy)
+
+    def seed_end(st):
+        for d in range(1, NZ):
+            zz = lax.rem(z + d, NZ)
+            ref = scal.at[st, zz]
+            pltpu.make_async_copy(ref, ref, scal_recv.at[st, zz]).wait()
+        table = jnp.concatenate([jnp.sum(scal[st], axis=0)] * 16, axis=0).T[0:SR]
+        ss, inner, token_grad = (
+            jnp.sum(jnp.where(lane_stream == i, table, 0.0), axis=1, keepdims=True)
+            for i in range(3)
+        )
+        last, head = last_rows(st)
+        factor = lax.rsqrt(ss / WIDTH + NORM_EPS)
+        token_grad = token_grad / CANDLEN
+        grad[st * SR : (st + 1) * SR] = (
+            token_grad * factor * head
+            - token_grad * factor * factor * factor * inner / WIDTH * last
+        ).astype(BF16)
+
     lax.fori_loop(0, NSEC, forward_step, 0)
+    seed_start(0)
     forward_end(1, jnp.int32(NSEC - 1))
-
-    slab = pl.ds(pl.multiple_of(z * SLAB, SLAB), SLAB)
-    head = lg_ref[:, slab] * sw_ref[:, slab]
-    last = states[NSEC].reshape(ROWS, SLAB).astype(F32)
-    ss = jnp.sum(last * last, axis=1, keepdims=True)
-    inner = jnp.sum(last * head, axis=1, keepdims=True)
-    rows = lax.broadcasted_iota(jnp.int32, (ROWS, 128), 0)
-    mine = jnp.logical_and(rows >= my_rows * TOK, rows < (my_rows + 1) * TOK)
-    token_grad = jnp.where(mine, cg_ref[0, sec * TOK // CANDLEN], 0.0)
-    table = jnp.where(
-        lane == 0, ss, jnp.where(lane == 1, inner, jnp.where(lane == 2, token_grad, 0.0))
-    )
-    if ROWS != 128:
-        table = jnp.concatenate([table] * (128 // ROWS), axis=0)
-    scal[z] = table.T[0:8]
-
-    def scal_copy(d):
-        zz, target = z_peer(d)
+    seed_start(1)
+    seed_end(0)
+
+    grad_rows = (pl.ds(0, RANK), pl.ds(RANK, GROWS - RANK))
+
+    def grad_copy(layer, q, pt):
         return pltpu.make_async_remote_copy(
-            src_ref=scal.at[z],
-            dst_ref=scal.at[z],
-            send_sem=scal_send.at[d],
-            recv_sem=scal_recv.at[z],
-            device_id=target,
-            device_id_type=MESH,
-        )
-
-    for d in range(1, NZ):
-        copy = scal_copy(d)
-        copy.start()
-        sends.append(copy)
-    for d in range(1, NZ):
-        zz = lax.rem(z + d, NZ)
-        pltpu.make_async_copy(scal.at[zz], scal.at[zz], scal_recv.at[zz]).wait()
-    table = jnp.concatenate([jnp.sum(scal[...], axis=0)] * 16, axis=0).T
-    if ROWS != 128:
-        table = table[0:ROWS]
-    ss = jnp.sum(jnp.where(lane == 0, table, 0.0), axis=1, keepdims=True)
-    inner = jnp.sum(jnp.where(lane == 1, table, 0.0), axis=1, keepdims=True)
-    token_grad = jnp.sum(jnp.where(lane == 2, table, 0.0), axis=1, keepdims=True)
-    factor = lax.rsqrt(ss / WIDTH + NORM_EPS)
-    token_grad = token_grad / CANDLEN
-    grad[...] = (
-        token_grad * factor * head
-        - token_grad * factor * factor * factor * inner / WIDTH * last
-    ).astype(BF16)
-
-    def grad_copy(layer, q):
-        return pltpu.make_async_remote_copy(
-            src_ref=grad_out.at[layer, q],
-            dst_ref=grad_in.at[my_slot],
-            send_sem=grad_send.at[layer, q],
-            recv_sem=grad_recv.at[my_slot],
+            src_ref=grad_out.at[layer, q, grad_rows[pt]],
+            dst_ref=grad_in.at[my_slot, grad_rows[pt]],
+            send_sem=grad_send.at[layer, q * 2 + pt],
+            recv_sem=grad_recv.at[my_slot, pt],
             device_id={"section": layer, "dp": z * 4 + q},
             device_id_type=MESH,
         )
+
+    def grad_leave(layer, q, pt):
+        here = jnp.logical_and(layer == sec, quarter == q)
+
+        @pl.when(jnp.logical_not(here))
+        def _():
+            grad_copy(layer, q, pt).start()
+
+        @pl.when(here)
+        def _():
+            grad_in[my_slot, grad_rows[pt]] = grad_out[layer, q, grad_rows[pt]]
 
     def backward_part(st, layer):
         value = jnp.zeros((SR, VW), F32)
         for q in range(4):
             value = value + dot_nt(
-                grad[st * SR : (st + 1) * SR, q * FB : (q + 1) * FB], weights[layer, q, 0:VW]
+                grad[st * SR : (st + 1) * SR, q * FB : (q + 1) * FB], weights[layer, q, R_O:R_B]
             )
         part[st, :, :, 0:VW] = value.astype(BF16).reshape(HALF, TOK, VW)
         exchange_start(st, 2 * NSEC - 1 - layer, VW)
@@ -572,9 +603,10 @@
             tail = forward_total[:, VW:PW]
             r = lax.rsqrt(get_scalar(tail, lane_own) / WIDTH + NORM_EPS)
             t = (r * tail[:, 0:RANK]).astype(BF16)
+            up_factor = ups(layer)
             dv = exchange_sum(st, step, VW).astype(BF16)
             dt32 = jnp.zeros((TOK, RANK), F32)
-            for w, up in enumerate(ups(layer)):
+            for w, up in enumerate(up_factor):
                 dt32 = dt32 + dot_nt(dv[:, w * FB : (w + 1) * FB], up)
             dt = (ADAPTER_SCALE * dt32).astype(BF16)
             dvf, dtf = dv.astype(F32), dt.astype(F32)
@@ -591,6 +623,7 @@
                     grad_out[layer, q, RANK + w * UPR : RANK + (w + 1) * UPR] = up_sum[
                         q * UPR : (q + 1) * UPR, w * FB : (w + 1) * FB
                     ]
+                grad_leave(layer, q, 1)
 
     def backward_end(st, layer):
         step = 2 * NSEC - 1 - layer
@@ -604,7 +637,7 @@
         def _():
             for q in range(4):
                 cols = slice(q * FB, (q + 1) * FB)
-                du = dot_nn(scaled, weights[layer, q, R_V:R_B])
+                du = dot_nn(scaled, weights[layer, q, R_V:R_G])
                 grad[own_rows, cols] = (
                     grad[own_rows, cols].astype(F32)
                     + du * gains(layer, q)
@@ -620,17 +653,10 @@
                 down_sums[q] = share
                 continue
             grad_out[layer, q, 0:RANK] = (down_sums[q] + share).astype(BF16)
-            here = jnp.logical_and(layer == sec, quarter == q)
-
-            @pl.when(jnp.logical_not(here))
-            def _():
-                grad_copy(layer, q).start()
-
-            @pl.when(here)
-            def _():
-                grad_in[my_slot] = grad_out[layer, q]
+            grad_leave(layer, q, 0)
 
     backward_part(0, jnp.int32(NSEC - 1))
+    seed_end(1)
 
     def backward_step(index, carry):
         layer = NSEC - 1 - index
@@ -660,17 +686,20 @@
     backward_end(1, jnp.int32(0))
     backward_sums(1, jnp.int32(0))
 
-    def collect(slot, carry):
-        @pl.when(slot != my_slot)
-        def _():
-            pltpu.make_async_copy(grad_in.at[slot], grad_in.at[slot], grad_recv.at[slot]).wait()
-
-        return carry
-
-    lax.fori_loop(0, NSEC * 4, collect, 0)
-    summed = jnp.sum(grad_in[...].astype(F32), axis=0)
-    up_z[z] = summed[RANK:GROWS].astype(BF16)
-    for d in range(1, NZ):
+    def collect(pt):
+        def wait_slot(slot, carry):
+            @pl.when(slot != my_slot)
+            def _():
+                ref = grad_in.at[slot, grad_rows[pt]]
+                pltpu.make_async_copy(ref, ref, grad_recv.at[slot, pt]).wait()
+
+            return carry
+
+        lax.fori_loop(0, NSEC * 4, wait_slot, 0)
+        return jnp.sum(grad_in[:, grad_rows[pt]].astype(F32), axis=0)
+
+    up_z[z] = collect(1).astype(BF16)
+    for d in far_first:
         zz, target = z_peer(d)
         copy = pltpu.make_async_remote_copy(
             src_ref=up_z.at[z],
@@ -682,7 +711,6 @@
         )
         copy.start()
         sends.append(copy)
-    gd_ref[...] = summed[0:RANK]
     for d in range(1, NZ):
         zz = lax.rem(z + d, NZ)
         pltpu.make_async_copy(up_z.at[zz], up_z.at[zz], up_recv.at[0, zz]).wait()
@@ -698,6 +726,7 @@
         )
         copy.start()
         sends.append(copy)
+    gd_ref[...] = collect(0)
     for d in range(1, 4):
         qq = lax.rem(quarter + d, 4)
         pltpu.make_async_copy(up_q.at[qq], up_q.at[qq], up_recv.at[1, qq]).wait()
@@ -709,21 +738,24 @@
 
     for copy in sends:
         copy.wait_send()
-    if NY > 1:
-        for copy in column_copies() + [column_relay(0), column_relay(1)]:
-            copy.wait_send()
-    for ys in range(NY):
-        for copy in row_copies(ys) + row_relays(ys):
-            copy.wait_send()
+    for pt in (0, 1):
+        if NY > 1:
+            for copy in column_copies(pt) + [column_relay(pt, 0), column_relay(pt, 1)]:
+                copy.wait_send()
+        for ys in range(NY):
+            for copy in row_copies(ys, pt) + [row_relay_copy(ys, pt, half) for half in (0, 1)]:
+                copy.wait_send()
 
     def drain(layer, carry):
         for lo in (0, 1):
-            core_copy(layer, lo).wait_send()
+            for pt in (0, 1):
+                core_copy(layer, lo, pt).wait_send()
         for q in range(4):
 
             @pl.when(jnp.logical_not(jnp.logical_and(layer == sec, quarter == q)))
             def _():
-                grad_copy(layer, q).wait_send()
+                for pt in (0, 1):
+                    grad_copy(layer, q, pt).wait_send()
 
         return carry
 
@@ -749,7 +781,7 @@
     rank = adapter_down_factor.shape[2]
     slab, rows = 4 * fb, nz * tok
     upr, qw = rank // 4, vw // fb
-    r_end = -(-(2 * vw + rank + upr * qw + 16) // 32) * 32
+    r_end = 2 * vw + rank + upr * qw + 32
     pw = vw + 128
     grows = rank + upr * qw
     cfg = (nsec, nz, tok, fb, vw, rank, width, cand_len)
@@ -774,25 +806,25 @@
             pltpu.VMEM((2 * nsec, nz, tok, pw), BF16),
             pltpu.VMEM((nsec, tok, pw), F32),
             pltpu.VMEM((4, rank, fb), F32),
-            pltpu.VMEM((nz, 8, 128), F32),
+            pltpu.VMEM((2, nz, 8, 128), F32),
             pltpu.VMEM((nsec, 4, grows, fb), BF16),
             pltpu.VMEM((nsec * 4, grows, fb), BF16),
             pltpu.VMEM((nz, upr * qw, fb), BF16),
             pltpu.VMEM((4, upr * qw, fb), F32),
-            dma((6,)),
-            dma((nsec // 2, 6)),
-            dma((nsec, 2)),
-            dma((nsec * 4, 2)),
+            dma((2, 6)),
+            dma((nsec, 6)),
+            dma((nsec, 4)),
+            dma((nsec * 4, 4)),
             dma((nz,)),
             dma((nz,)),
             dma((2, nz)),
             dma((nz,)),
             dma((nz,)),
             dma((nz,)),
-            dma((nz,)),
-            dma((nz,)),
-            dma((nsec, 4)),
-            dma((nsec * 4,)),
+            dma((2, nz)),
+            dma((2, nz)),
+            dma((nsec, 8)),
+            dma((nsec * 4, 2)),
             dma((2, 8)),
             dma((2, 8)),
         ],

time: 297 us -> 263 us (0.89)
  Pallas kernels: 293 us -> 259 us
    pallas_call x1, Pallas kernels: 293 us -> 259 us  [per_device(): pl.pallas_call(functools.partial(kernel, cfg), out_shape=(jax.ShapeDtypeS...]
where the time goes in v4:
time: 263 us
  Pallas kernels  259 us (98%)
  local copies, waits for them, and re-layouts  3.04 us (1%)
    pallas_call x1, Pallas kernels, per_device(): pl.pallas_call(functools.partial(kernel, cfg), out_shape=(jax.ShapeDtypeS...  259 us

profile of v4, /device:TPU:1, one launch (start us, length us, event | category | flops | bytes accessed | tf_op | source)
XLA Modules:
  0.0 263.0 jit_solution(8620853871198301784)
XLA Ops:
  0.6 259.3 %layers.1 = (f32[64,256]{1,0:T(8,128)}, f32[64,512]{1,0:T(8,128)}) custom-call(bf16[128,8192]{1,0:T(8,128)(2,1)} %bitcast.14, bf16[512,256]{1,0:T(8,128)(2,1)} %bitcast.15, bf16[256,512]{1,0:T(8,128)(2,1)} %bitcast.16, bf16[64,256]{1,0:T(8,128)(2,1)} %bitcast.20, bf16[64,512]{1,0:T(8,128)(2,1)} %bitcast.18, f32[1,8192]{1,0:T(1,128)} %g_ref.1, ...), custom_call_target="tpu_custom_call" | custom-call | tf_op jit(solution)/shard_map/layers/pallas_call | solution.py:790
  259.9 1.5 copy.13
  261.4 1.6 copy.14

commit v5 on v4

--- a/solution.py
+++ b/solution.py
@@ -61,6 +61,7 @@
     up_q,
     own_send,
     relay_send,
+    wide_send,
     core_send,
     weight_recv,
     h_send,
@@ -255,6 +256,49 @@
             weight_wait(k, q, pt, half)
             row_relay_copy(ys, pt, half).start()
 
+    def wide_copies(xs):
+        up, down = device(x, y_next, z, core), device(x, y_prev, z, core)
+        return [
+            weight_copy(xs, y, 1, half, target, wide_send.at[xs, i])
+            for i, (half, target) in enumerate(((0, up), (1, down), (1, up), (0, down)))
+        ]
+
+    def wide_relay(xs, half):
+        source, target = (y_prev, y_next) if half == 0 else (y_next, y_prev)
+        target = device(x, target, z, core)
+        return weight_copy(xs, source, 1, half, target, wide_send.at[xs, 4 + half])
+
+    def wide_send_all():
+        row_relay(y, 1)
+        for source, half in ((x_prev, 1), (x_next, 0)):
+            k, q = place(source, y, core)
+            weight_wait(k, q, 1, half)
+        k, q = place(lax.rem(x + 2, NX), y, core)
+        for half in (0, 1):
+            weight_wait(k, q, 1, half)
+        for xs in range(NX):
+            for copy in wide_copies(xs):
+                copy.start()
+
+    def wide_near(ys):
+        for half, source in ((0, y_prev), (1, y_next)):
+
+            @pl.when(source == ys)
+            def _():
+                for xs in range(NX):
+                    k, q = place(xs, ys, core)
+                    weight_wait(k, q, 1, half)
+                    wide_relay(xs, half).start()
+
+    def wide_rest(ys):
+        for half, source in ((0, y_prev), (1, y_next)):
+
+            @pl.when(jnp.logical_and(y != ys, source != ys))
+            def _():
+                for xs in range(NX):
+                    k, q = place(xs, ys, core)
+                    weight_wait(k, q, 1, half)
+
     def core_copy(layer, lo, pt):
         q = lo * 2 + core
         rows = pl.ds(STARTS[pt], 2 * SIZES[pt])
@@ -272,11 +316,13 @@
             xs = (layer % 2) * 2 + lo
             q = lo * 2 + core
 
-            @pl.when(jnp.logical_and(xs != x, xs != x_prev))
+            narrow = jnp.logical_or(layer < 2, pt == 0)
+
+            @pl.when(jnp.logical_and(narrow, jnp.logical_and(xs != x, xs != x_prev)))
             def _():
                 weight_wait(layer, q, pt, 0)
 
-            @pl.when(jnp.logical_and(xs != x, xs != x_next))
+            @pl.when(jnp.logical_and(narrow, jnp.logical_and(xs != x, xs != x_next)))
             def _():
                 weight_wait(layer, q, pt, 1)
 
@@ -299,8 +345,9 @@
 
     @pl.when(y != 0)
     def _():
-        for copy in column_copies(0) + column_copies(1):
+        for copy in column_copies(0):
             copy.start()
+        row_send(y, 1)
 
     row_relay(0, 0)
 
@@ -461,10 +508,13 @@
     forward_part(0, jnp.int32(0))
     row_relay(0, 1)
     for ys in range(1, NY):
-        for pt in (0, 1):
-            column(ys, pt)
-            if ys == 1:
-                row_send(ys, pt)
+        column(ys, 0)
+        if ys == 1:
+            row_send(ys, 0)
+
+    @pl.when(y != 0)
+    def _():
+        wide_send_all()
 
     def forward_step(layer, carry):
         @pl.when(layer > 0)
@@ -473,12 +523,15 @@
 
         forward_part(1, layer)
 
+        @pl.when(jnp.logical_and(layer % 2 == 0, layer > 0))
+        def _():
+            wide_rest(layer // 2)
+
         pass_on(layer, 1)
 
         @pl.when(jnp.logical_and(layer % 2 == 1, (layer + 3) // 2 < NY))
         def _():
-            for pt in (0, 1):
-                row_send((layer + 3) // 2, pt)
+            row_send((layer + 3) // 2, 0)
 
         take_over(layer, 1)
         forward_own(0, layer)
@@ -486,8 +539,8 @@
 
         @pl.when(jnp.logical_and(layer % 2 == 0, layer // 2 + 1 < NY))
         def _():
-            for pt in (0, 1):
-                row_relay(layer // 2 + 1, pt)
+            row_relay(layer // 2 + 1, 0)
+            wide_near(layer // 2 + 1)
 
         @pl.when(layer + 1 < NSEC)
         def _():
@@ -738,13 +791,39 @@
 
     for copy in sends:
         copy.wait_send()
-    for pt in (0, 1):
-        if NY > 1:
-            for copy in column_copies(pt) + [column_relay(pt, 0), column_relay(pt, 1)]:
+    def row_done(ys, pt):
+        for copy in row_copies(ys, pt) + [row_relay_copy(ys, pt, half) for half in (0, 1)]:
+            copy.wait_send()
+
+    for ys in range(NY):
+        row_done(ys, 0)
+    row_done(0, 1)
+    if NY > 1:
+        for copy in column_copies(0) + [column_relay(0, 0), column_relay(0, 1)]:
+            copy.wait_send()
+
+        @pl.when(y == 0)
+        def _():
+            for copy in column_copies(1):
                 copy.wait_send()
-        for ys in range(NY):
-            for copy in row_copies(ys, pt) + [row_relay_copy(ys, pt, half) for half in (0, 1)]:
-                copy.wait_send()
+
+        @pl.when(y != 0)
+        def _():
+            row_done(y, 1)
+            for xs in range(NX):
+                for copy in wide_copies(xs):
+                    copy.wait_send()
+
+        for half, source in ((0, y_prev), (1, y_next)):
+
+            @pl.when(source == 0)
+            def _():
+                column_relay(1, half).wait_send()
+
+            @pl.when(source != 0)
+            def _():
+                for xs in range(NX):
+                    wide_relay(xs, half).wait_send()
 
     def drain(layer, carry):
         for lo in (0, 1):
@@ -813,6 +892,7 @@
             pltpu.VMEM((4, upr * qw, fb), F32),
             dma((2, 6)),
             dma((nsec, 6)),
+            dma((4, 6)),
             dma((nsec, 4)),
             dma((nsec * 4, 4)),
             dma((nz,)),

time: 263 us -> 284 us (1.080)
  Pallas kernels: 259 us -> 280 us
    pallas_call x1, Pallas kernels: 259 us -> 280 us  [per_device(): pl.pallas_call(functools.partial(kernel, cfg), out_shape=(jax.ShapeDtypeS...]
where the time goes in v5:
time: 284 us; the launch traced here: 283 us
  Pallas kernels  280 us (99%)
  local copies, waits for them, and re-layouts  3.04 us (1%)
    pallas_call x1, Pallas kernels, per_device(): pl.pallas_call(functools.partial(kernel, cfg), out_shape=(jax.ShapeDtypeS...  280 us

profile of v5, /device:TPU:1, one launch (start us, length us, event | category | flops | bytes accessed | tf_op | source)
XLA Modules:
  0.0 283.4 jit_solution(9821415567805076960)
XLA Ops:
  0.6 279.7 %layers.1 = (f32[64,256]{1,0:T(8,128)}, f32[64,512]{1,0:T(8,128)}) custom-call(bf16[128,8192]{1,0:T(8,128)(2,1)} %bitcast.14, bf16[512,256]{1,0:T(8,128)(2,1)} %bitcast.15, bf16[256,512]{1,0:T(8,128)(2,1)} %bitcast.16, bf16[64,256]{1,0:T(8,128)(2,1)} %bitcast.20, bf16[64,512]{1,0:T(8,128)(2,1)} %bitcast.18, f32[1,8192]{1,0:T(1,128)} %g_ref.1, ...), custom_call_target="tpu_custom_call" | custom-call | tf_op jit(solution)/shard_map/layers/pallas_call | solution.py:869
  280.3 1.5 copy.13
  281.8 1.6 copy.14

commit v6 on v4

--- a/solution.py
+++ b/solution.py
@@ -460,8 +460,8 @@
     take_over(jnp.int32(0), 0)
     forward_part(0, jnp.int32(0))
     row_relay(0, 1)
-    for ys in range(1, NY):
-        for pt in (0, 1):
+    for pt in (0, 1):
+        for ys in range(1, NY):
             column(ys, pt)
             if ys == 1:
                 row_send(ys, pt)
@@ -475,6 +475,10 @@
 
         pass_on(layer, 1)
 
+        @pl.when(jnp.logical_and(layer % 2 == 1, (layer + 1) // 2 < NY))
+        def _():
+            row_relay((layer + 1) // 2, 1)
+
         @pl.when(jnp.logical_and(layer % 2 == 1, (layer + 3) // 2 < NY))
         def _():
             for pt in (0, 1):
@@ -486,8 +490,7 @@
 
         @pl.when(jnp.logical_and(layer % 2 == 0, layer // 2 + 1 < NY))
         def _():
-            for pt in (0, 1):
-                row_relay(layer // 2 + 1, pt)
+            row_relay(layer // 2 + 1, 0)
 
         @pl.when(layer + 1 < NSEC)
         def _():

time: 263 us -> 261 us (level)
  no operation moved by 1% of the time
where the time goes in v6:
time: 261 us
  Pallas kernels  257 us (98%)
  local copies, waits for them, and re-layouts  3.04 us (1%)
    pallas_call x1, Pallas kernels, per_device(): pl.pallas_call(functools.partial(kernel, cfg), out_shape=(jax.ShapeDtypeS...  257 us

profile of v6, /device:TPU:1, one launch (start us, length us, event | category | flops | bytes accessed | tf_op | source)
XLA Modules:
  0.0 261.1 jit_solution(11596238759125025464)
XLA Ops:
  0.6 257.5 %layers.1 = (f32[64,256]{1,0:T(8,128)}, f32[64,512]{1,0:T(8,128)}) custom-call(bf16[128,8192]{1,0:T(8,128)(2,1)} %bitcast.14, bf16[512,256]{1,0:T(8,128)(2,1)} %bitcast.15, bf16[256,512]{1,0:T(8,128)(2,1)} %bitcast.16, bf16[64,256]{1,0:T(8,128)(2,1)} %bitcast.20, bf16[64,512]{1,0:T(8,128)(2,1)} %bitcast.18, f32[1,8192]{1,0:T(1,128)} %g_ref.1, ...), custom_call_target="tpu_custom_call" | custom-call | tf_op jit(solution)/shard_map/layers/pallas_call | solution.py:793
  258.1 1.5 copy.13
  259.6 1.6 copy.14
